TPU v7x, 256 devices: a whole 4x4x8 slice. The times are simulated.
256 devices in a mesh: dp: 32 (over z_hi, y, core), seq: 8 (over z_lo, x).
Axes of the slice: x: 4, y: 4, z: 8 (z_hi: 4, z_lo: 2; z = z_hi * 2 + z_lo), core: 2. Of those that a mesh axis runs over, the one named last changes fastest.
Arguments:
- layer_input: bfloat16 [32768, 4096], P(('dp', 'seq')), may hold values from -24 to 24
- queries: bfloat16 [32768, 2048], P(('dp', 'seq')), may hold values from -24 to 24
- key_rows: bfloat16 [32768, 2048], P(('dp', 'seq')), may hold values from -24 to 24
- value_rows: bfloat16 [32768, 2048], P(('dp', 'seq')), may hold values from -6 to 6
- output_grad: bfloat16 [32768, 4096], P(('dp', 'seq')), may hold values from -24 to 24
- out_weight: bfloat16 [2048, 4096], P('seq', 'dp'), may hold values from -0.125 to 0.125
- segment_ids: int32 [32, 1024], P('dp', 'seq'), may hold values from 0 to 3, never falling along the last dimension, each value on 1 to 512 neighbouring positions
- timesteps: int32 [32], P('dp'), may hold values from 125 to 1000
- masked_tokens: int32 [32768], P(('dp', 'seq')), may hold values 0 or 1
Outputs:
- grad_query: float32 [4096, 2048], P('dp', 'seq')
- grad_key: float32 [4096, 2048], P('dp', 'seq')
- grad_value: float32 [4096, 2048], P('dp', 'seq')
- grad_out: float32 [2048, 4096], P('seq', 'dp')
All inputs are finite; a program needn't handle non-finite values. No bound on the sum of `masked_tokens` on one device may be relied on, other than what follows from the above.
Results may differ from a plain program's by a relative error of at most 0.024.
Values may be sent and summed in bfloat16 or wider, within the bound.
No kernel may reach another device: no remote copies, remote signals or barrier semaphores. Data moves between devices by JAX's collectives and lax.ppermute only.
A program may use at most 128 MiB of HBM per device.

v0:
```python
import jax
import jax.numpy as jnp
from jax import lax
from jax.experimental import pallas as pl
from jax.experimental.pallas import tpu as pltpu
from jax.sharding import Mesh, PartitionSpec as P

HEAD = 128
TSTEPS = 1000
TOK = 128
AXES = ("h", "y", "c", "l", "x")
SIZES = (4, 4, 2, 2, 4)
DP = ("h", "y", "c")
SEQ = ("l", "x")
RELATIVE = [(dl, dx) for dl in range(2) for dx in range(4)]
HALF = 2048
F32, BF16 = jnp.float32, jnp.bfloat16
VMEM = pl.BlockSpec(memory_space=pltpu.VMEM)
SMEM = pl.BlockSpec(memory_space=pltpu.SMEM)
HBM = pl.BlockSpec(memory_space=pltpu.HBM)


def recv(block, axis, offset):
    n = SIZES[AXES.index(axis)]
    return lax.ppermute(block, axis, [((i + offset) % n, i) for i in range(n)])


def send_zz(block, target, only=None):
    pairs = []
    for h in range(4):
        for l in range(2):
            if only is None or only == h // 2:
                h1, h0, to_l = target(h // 2, h % 2, l)
                pairs.append((h * 2 + l, (h1 * 2 + h0) * 2 + to_l))
    return lax.ppermute(block, ("h", "l"), pairs)


def ring(block):
    near, far, across = recv(block, "x", 1), recv(block, "x", 3), recv(block, "x", 2)
    return [block, near, across, far]


def dot(a, b, dims):
    return lax.dot_general(a, b, (dims, ((), ())), preferred_element_type=F32)


def call(kernel, name, inputs, specs, out_shape, out_specs, deps=(), grid=(1,), scratch=()):
    n, m = len(inputs), len(deps)

    def body(*refs):
        kernel(*refs[:n], *refs[n + m :])

    def whole(spec, array):
        zeros = (0,) * len(array.shape)
        return pl.BlockSpec(array.shape, lambda i: zeros) if spec is VMEM else spec

    outs = out_shape if isinstance(out_shape, tuple) else (out_shape,)
    out_specs = out_specs if isinstance(out_specs, tuple) else (out_specs,)
    results = pl.pallas_call(
        body,
        grid=grid,
        out_shape=outs,
        in_specs=[whole(s, a) for s, a in zip(specs, inputs)] + [HBM] * m,
        out_specs=tuple(whole(s, a) for s, a in zip(out_specs, outs)),
        scratch_shapes=scratch,
        compiler_params=pltpu.CompilerParams(vmem_limit_bytes=60 * 2**20),
        cost_estimate=pl.CostEstimate(flops=0, bytes_accessed=0, transcendentals=0),
        name=name,
    )(*inputs, *deps)
    return results if isinstance(out_shape, tuple) else results[0]


def gate(x, deps):
    return pl.pallas_call(
        lambda *refs: None,
        out_shape=jax.ShapeDtypeStruct(x.shape, x.dtype),
        in_specs=[HBM] * (1 + len(deps)),
        out_specs=HBM,
        input_output_aliases={0: 0},
        cost_estimate=pl.CostEstimate(flops=0, bytes_accessed=0, transcendentals=0),
        name="gate",
    )(x, *deps)


def shape(*dims, dtype=BF16):
    return jax.ShapeDtypeStruct(dims, dtype)


def scale_kernel(place_ref, g_ref, w_ref, keep_ref, send_ref):
    w = w_ref[...]
    mine = pl.multiple_of(place_ref[3] * HALF, HALF)
    other = pl.multiple_of((1 - place_ref[3]) * HALF, HALF)
    keep_ref[...] = (g_ref[:, pl.ds(mine, HALF)].astype(F32) * w).astype(BF16)
    send_ref[...] = (g_ref[:, pl.ds(other, HALF)].astype(F32) * w).astype(BF16)


def pack_kernel(q_ref, k_ref, v_ref, s_ref, o_ref):
    segs = jnp.broadcast_to(s_ref[...].astype(F32), (16, TOK)).astype(BF16)
    for dest in range(8):
        for head in range(2):
            cols = slice((dest * 2 + head) * HEAD, (dest * 2 + head + 1) * HEAD)
            for j, ref in enumerate((q_ref, k_ref, v_ref)):
                at = slice((head * 3 + j) * HEAD, (head * 3 + j + 1) * HEAD)
                o_ref[dest, :TOK, at] = ref[:, cols]
                o_ref[dest, TOK:, at] = segs


def reorder_kernel(order_ref, x_ref, *o_refs):
    for i, ref in enumerate(o_refs):
        for j in range(16):
            start = pl.multiple_of(order_ref[i * 16 + j] * 128, 128)
            ref[:, j * 128 : (j + 1) * 128] = x_ref[:, pl.ds(start, 128)]


def pair_kernel(a_ref, b_ref, o_ref):
    o_ref[:TOK] = a_ref[...]
    o_ref[TOK:] = b_ref[...]


def load_rows(x_ref, idx_ref, part):
    cols = slice(part * HEAD, (part + 1) * HEAD)
    return jnp.concatenate([x_ref[idx_ref[r], :TOK, cols] for r in range(8)], axis=0)


def forward_kernel(idx_ref, x_ref, att_ref, p_ref):
    factor = HEAD ** (-0.5)
    keys = load_rows(x_ref, idx_ref, 1)
    values = load_rows(x_ref, idx_ref, 2)
    segs = [x_ref[idx_ref[r], TOK : TOK + 16, :HEAD].astype(F32)[:1] for r in range(8)]
    seg_row = jnp.concatenate(segs, axis=1)
    for blk in range(8):
        rows = slice(blk * TOK, (blk + 1) * TOK)
        q = x_ref[idx_ref[blk], :TOK, :HEAD]
        seg_col = jnp.broadcast_to(segs[blk], (TOK, TOK)).T[:, :1]
        scores = dot(q, keys, ((1,), (1,))) * factor
        scores = jnp.where(seg_col == seg_row, scores, -jnp.inf)
        shifted = jnp.exp(scores - jnp.max(scores, axis=-1, keepdims=True))
        probs = shifted * (1.0 / jnp.sum(shifted, axis=-1, keepdims=True))
        low = probs.astype(BF16)
        p_ref[0, rows, :] = low
        att_ref[:, rows] = dot(low, values, ((1,), (0,))).T.astype(BF16)


def backward_kernel(idx_ref, x_ref, p_ref, dout_ref, o_ref, dk_ref, dv_ref):
    factor = HEAD ** (-0.5)
    keys = load_rows(x_ref, idx_ref, 1)
    values = load_rows(x_ref, idx_ref, 2)
    for blk in range(4):
        rows = slice(blk * 256, (blk + 1) * 256)
        q = jnp.concatenate([x_ref[idx_ref[2 * blk + j], :TOK, :HEAD] for j in range(2)], axis=0)
        low = p_ref[0, rows, :]
        dout = dout_ref[rows, :]
        dprobs = dot(dout, values, ((1,), (1,)))
        probs = low.astype(F32)
        delta = jnp.sum(probs * dprobs, axis=-1, keepdims=True)
        dscores = (probs * (dprobs - delta) * factor).astype(BF16)
        o_ref[:HEAD, rows] = dot(dscores, keys, ((1,), (0,))).T.astype(BF16)
        dk = dot(q, dscores, ((0,), (0,)))
        dv = dot(dout, low, ((0,), (0,)))
        if blk == 0:
            dk_ref[...] = dk
            dv_ref[...] = dv
        else:
            dk_ref[...] += dk
            dv_ref[...] += dv
    o_ref[HEAD : 2 * HEAD, :] = dk_ref[...].astype(BF16)
    o_ref[2 * HEAD :, :] = dv_ref[...].astype(BF16)


def flipped(lhs):
    return jnp.concatenate([lhs[:, 512:], lhs[:, :512]], axis=1)


def by_x(lhs_ref, x, flip):
    blocks = []
    for at_x in range(4):
        for dl in range(2):
            row = (1 - dl if flip else dl) * 4 + (at_x - x + 4) % 4
            blocks.append(lhs_ref[:, pl.ds(pl.multiple_of(row * TOK, TOK), TOK)])
    return jnp.concatenate(blocks, axis=1)


def dout_kernel(*refs):
    pieces, (w_ref, place_ref, keep_ref, send_ref) = refs[:8], refs[8:]
    mine = pl.multiple_of(place_ref[3] * HALF, HALF)
    other = pl.multiple_of((1 - place_ref[3]) * HALF, HALF)
    for quarter in range(4):
        left = jnp.concatenate([p[...] for p in pieces[2 * quarter : 2 * quarter + 2]], axis=0)
        rows = slice(quarter * 256, (quarter + 1) * 256)
        keep_ref[rows, :] = dot(left, w_ref[:, pl.ds(mine, HALF)], ((1,), (1,)))
        at = (quarter + 2) % 4 * 256
        total = dot(left, w_ref[:, pl.ds(other, HALF)], ((1,), (1,)))
        send_ref[at : at + 256, :] = total.astype(BF16)


def out_terms_kernel(*refs):
    pieces, (own_ref, other_ref, place_ref, send_ref, keep_ref) = refs[:8], refs[8:]
    h0, c = place_ref[0] % 2, place_ref[2]
    att = jnp.concatenate([own_ref[...], flipped(other_ref[...])], axis=0)
    for tile in range(8):
        cols = slice(tile * 256, (tile + 1) * 256)
        rhs = jnp.concatenate([p[:, cols] for p in pieces], axis=0)
        term = dot(att, rhs, ((1,), (0,))).astype(BF16)
        at = tile % 4
        a = (tile // 4 + h0) % 2
        send_ref[at, a] = jnp.where(c == 0, term[:, 128:], term[:, :128])
        keep_ref[at, a] = jnp.where(c == 0, term[:, :128], term[:, 128:])


def term_blocks(lhs, slab, place, flip, deps):
    n, m = len(lhs), sum(a.shape[0] for a in lhs)

    def kernel(*refs):
        slab_ref, place_ref, send_ref, keep_ref = refs[n:]
        left = jnp.concatenate([by_x(r, place_ref[4], flip) for r in refs[:n]], axis=0)
        for tile in range(8):
            cols = slice(tile * 256, (tile + 1) * 256)
            term = dot(left, slab_ref[:, cols], ((1,), (0,))).astype(BF16)
            out = send_ref if tile % 4 < 2 else keep_ref
            out[(tile % 2) * 2, tile // 4] = term[:, :128]
            out[(tile % 2) * 2 + 1, tile // 4] = term[:, 128:]

    return call(
        kernel,
        "term_blocks",
        list(lhs) + [slab, place],
        [VMEM] * (n + 1) + [SMEM],
        (shape(4, 2, m, 128), shape(4, 2, m, 128)),
        (VMEM, VMEM),
        deps=deps,
    )


def finish_kernel(*refs):
    for head in range(2):
        for j in range(3):
            rows = slice((head * 3 + j) * HEAD, (head * 3 + j + 1) * HEAD)
            total = sum(r[rows, :].astype(F32) for r in refs[:8])
            refs[8 + j][:, head * HEAD : (head + 1) * HEAD] = total.T


def add_low(a, b):
    return (a.astype(F32) + b.astype(F32)).astype(BF16)


def shards(
    layer_input,
    queries,
    key_rows,
    value_rows,
    output_grad,
    out_weight,
    segment_ids,
    timesteps,
    masked_tokens,
):
    total_tokens = layer_input.shape[0] * 256
    norm_scale = float(total_tokens) ** (-0.5)
    h, y, c, l, x = (lax.axis_index(a) for a in AXES)
    idx = jnp.stack([((l + dl) % 2) * 4 + (x + dx) % 4 for dl, dx in RELATIVE]).astype(jnp.int32)
    place = jnp.stack([h, y, c, l, x]).astype(jnp.int32)

    out_rows = send_zz(out_weight, lambda h1, h0, to_l: (to_l, h0, h1))
    out_rows = lax.all_gather(out_rows, DP, axis=1, tiled=True)

    row_weight = masked_tokens.astype(F32) * (TSTEPS / timesteps.astype(F32)) * norm_scale
    scaled_keep, scaled_send = call(
        scale_kernel,
        "scale",
        [place, output_grad, row_weight[:, None]],
        [SMEM, VMEM, VMEM],
        (shape(TOK, HALF), shape(TOK, HALF)),
        (VMEM, VMEM),
    )
    scaled_pair = recv(scaled_send, "l", 1)
    scaled = ring(scaled_keep)
    order = [
        ((half * 2 + (h + a) % 2) * 4 + at_y) * 2 + (c + dc) % 2
        for half in (l, 1 - l)
        for a in (1, 0)
        for dc in (1, 0)
        for at_y in range(4)
    ]
    layer_keep, layer_send = call(
        reorder_kernel,
        "reorder",
        [jnp.stack(order).astype(jnp.int32), layer_input],
        [SMEM, VMEM],
        (shape(TOK, HALF),) * 2,
        (VMEM,) * 2,
        deps=[scaled_keep],
    )
    layer_pair = recv(layer_send, "l", 1)

    to_heads = call(
        pack_kernel,
        "pack",
        [queries, key_rows, value_rows, segment_ids],
        [VMEM] * 4,
        shape(8, TOK + 16, 768),
        VMEM,
        deps=[scaled_keep],
    )
    packed = lax.all_to_all(to_heads, SEQ, split_axis=0, concat_axis=0, tiled=True)
    scaled = scaled + ring(gate(scaled_pair, [packed] + scaled[1:]))

    attended, probs = call(
        forward_kernel,
        "attention_forward",
        [idx, packed],
        [SMEM, pl.BlockSpec((8, TOK + 16, 384), lambda i: (0, 0, i))],
        (shape(256, 1024), shape(2, 1024, 1024)),
        (
            pl.BlockSpec((HEAD, 1024), lambda i: (i, 0)),
            pl.BlockSpec((1, 1024, 1024), lambda i: (i, 0, 0)),
        ),
        grid=(2,),
    )
    attended_pair = recv(attended, "l", 1)
    layer = call(
        pair_kernel,
        "pair",
        [layer_keep, layer_pair],
        [VMEM, VMEM],
        shape(2 * TOK, HALF),
        VMEM,
        deps=[attended] + scaled[5:],
    )
    slab = lax.all_gather(layer, "x", axis=0, tiled=True)
    dout_keep, dout_send = call(
        dout_kernel,
        "dout",
        scaled + [out_rows, place],
        [VMEM] * 9 + [SMEM],
        (shape(1024, 256, dtype=F32), shape(1024, 256)),
        (VMEM, VMEM),
        deps=[layer],
    )
    dout = (dout_keep + recv(dout_send, "l", 1).astype(F32)).astype(BF16)

    out_send, out_keep = call(
        out_terms_kernel,
        "out_terms",
        scaled + [attended, attended_pair, place],
        [VMEM] * 10 + [SMEM],
        (shape(4, 2, 512, 128), shape(4, 2, 512, 128)),
        (VMEM, VMEM),
        deps=[dout_send],
    )

    def backward(head, deps):
        return call(
            backward_kernel,
            "attention_backward",
            [idx, packed, probs, dout],
            [
                SMEM,
                pl.BlockSpec((8, TOK + 16, 384), lambda i: (0, 0, head)),
                pl.BlockSpec((1, 1024, 1024), lambda i: (head, 0, 0)),
                pl.BlockSpec((1024, HEAD), lambda i: (0, head)),
            ],
            shape(384, 1024),
            pl.BlockSpec((384, 1024), lambda i: (0, 0)),
            deps=deps,
            scratch=[pltpu.VMEM((HEAD, 1024), F32), pltpu.VMEM((HEAD, 1024), F32)],
        )

    terms_t = [backward(0, [out_keep])]
    terms_t.append(backward(1, [terms_t[0]]))
    terms_pair = [recv(t, "l", 1) for t in terms_t]

    def core_sum(send, keep):
        return add_low(keep, recv(send, "c", 1))

    def y_sum(blocks):
        arrived = lax.all_to_all(blocks, "y", split_axis=0, concat_axis=0, tiled=True)
        return jnp.sum(arrived.astype(F32), axis=0).astype(BF16)

    out_blocks = core_sum(gate(out_send, [terms_t[1]]), out_keep)
    out_part = y_sum(out_blocks)
    grad_out = 0.0
    for a in range(2):
        for b in range(2):
            chosen = lax.dynamic_slice_in_dim(out_part[a], (h // 2 + b + l) % 2 * 256, 256, 0)
            chosen = send_zz(chosen, lambda h1, h0, l: (l, h0 ^ a, h1 ^ b))
            grad_out = grad_out + chosen.astype(F32)

    deps = [out_part, terms_pair[0]]
    blocks = core_sum(*term_blocks(terms_t, slab, place, False, deps))
    part = y_sum(blocks)
    full = []
    for i, a in enumerate((1, 0)):
        for s in range(2):
            full.append(send_zz(part[i], lambda h1, h0, l: (l, h0 ^ a, l), s))
    blocks = core_sum(*term_blocks(terms_pair, slab, place, True, [part]))
    part = gate(y_sum(blocks), [grad_out] + full)
    for i, a in enumerate((1, 0)):
        for s in range(2):
            full.append(send_zz(part[i], lambda h1, h0, l: (l, h0 ^ a, 1 - l), s))
    grad_q, grad_k, grad_v = call(
        finish_kernel,
        "finish",
        full,
        [VMEM] * 8,
        tuple(shape(128, 256, dtype=F32) for _ in range(3)),
        (VMEM,) * 3,
    )
    return grad_q, grad_k, grad_v, grad_out


def solution(mesh):
    view = Mesh(mesh.devices.reshape(SIZES), AXES)
    tokens = P(DP + SEQ, None)
    return jax.shard_map(
        shards,
        mesh=view,
        in_specs=(
            tokens,
            tokens,
            tokens,
            tokens,
            tokens,
            P(SEQ, DP),
            P(DP, SEQ),
            P(DP),
            P(DP + SEQ),
        ),
        out_specs=(P(DP, SEQ), P(DP, SEQ), P(DP, SEQ), P(SEQ, DP)),
        check_vma=False,
    )
```

profile of v0, /device:TPU:104, one launch (start us, length us, event | category | flops | bytes accessed | tf_op | source)
XLA Modules:
  0.0 297.1 jit_solution(7584309660893355424)
XLA Ops:
  7.2 5.9 %collective-permute-start.7 = (bf16[256,128]{1,0:T(8,128)(2,1)}, bf16[256,128]{1,0:T(8,128)(2,1)S(1)}, u32[]{:S(2)}, u32[]{:S(2)}) collective-permute-start(bf16[256,128]{1,0:T(8,128)(2,1)} %param.14), channel_id=1, source_target_pairs={{0,0},{4,128},{64,64},{68,192},{128,4},{132,132},{192,68},{196,196... | collective-permute-start | bytes 196616 | tf_op jit(solution)/shard_map/ppermute | solution.py:35
  13.2 3.4 %collective-permute-done.7 = bf16[256,128]{1,0:T(8,128)(2,1)S(1)} collective-permute-done((bf16[256,128]{1,0:T(8,128)(2,1)}, bf16[256,128]{1,0:T(8,128)(2,1)S(1)}, u32[]{:S(2)}, u32[]{:S(2)}) %collective-permute-start.7) | collective-permute-done | bytes 65568 | tf_op jit(solution)/shard_map/ppermute | solution.py:35
  25.3 5.9 %all-to-all-start = ((bf16[8,144,768]{2,1,0:T(8,128)(2,1)}), bf16[8,144,768]{2,1,0:T(8,128)(2,1)S(1)}, u32[]{:S(2)}, u32[]{:S(2)}) async-start(bf16[8,144,768]{2,1,0:T(8,128)(2,1)} %pack.1), calls=%async_computation | async-start | bytes 3538944 | tf_op jit(solution)/shard_map/all_to_all | solution.py:304
  40.8 21.2 %collective-permute-done.refs_2_.refs_1_ = bf16[128,2048]{1,0:T(8,128)(2,1)S(1)} collective-permute-done((bf16[128,2048]{1,0:T(8,128)(2,1)S(1)}, bf16[128,2048]{1,0:T(8,128)(2,1)S(1)}, u32[]{:S(2)}, u32[]{:S(2)}) %collective-permute-start) | collective-permute-done | bytes 524320 | tf_op jit(solution)/shard_map/ppermute | solution.py:25
  62.1 4.0 %collective-permute-done.1.refs_3_.refs_2_ = bf16[128,2048]{1,0:T(8,128)(2,1)S(1)} collective-permute-done((bf16[128,2048]{1,0:T(8,128)(2,1)S(1)}, bf16[128,2048]{1,0:T(8,128)(2,1)S(1)}, u32[]{:S(2)}, u32[]{:S(2)}) %collective-permute-start.1) | collective-permute-done | bytes 524320 | tf_op jit(solution)/shard_map/ppermute | solution.py:25
  66.1 8.5 %collective-permute-done.2.refs_4_.refs_3_ = bf16[128,2048]{1,0:T(8,128)(2,1)} collective-permute-done((bf16[128,2048]{1,0:T(8,128)(2,1)S(1)}, bf16[128,2048]{1,0:T(8,128)(2,1)}, u32[]{:S(2)}, u32[]{:S(2)}) %collective-permute-start.2) | collective-permute-done | bytes 524320 | tf_op jit(solution)/shard_map/ppermute | solution.py:25
  80.1 10.3 %attention_forward.1 = (bf16[256,1024]{1,0:T(8,128)(2,1)}, bf16[2,1024,1024]{2,1,0:T(8,128)(2,1)}) custom-call(s32[8]{0:T(128)} %stack.152.refs_0_, bf16[8,144,768]{2,1,0:T(8,128)(2,1)} %copy-done), custom_call_target="tpu_custom_call" | custom-call | tf_op jit(solution)/shard_map/attention_forward/pallas_call | solution.py:59
  90.4 10.6 %collective-permute-done.4.refs_3_.refs_5_ = bf16[128,2048]{1,0:T(8,128)(2,1)S(1)} collective-permute-done((bf16[128,2048]{1,0:T(8,128)(2,1)}, bf16[128,2048]{1,0:T(8,128)(2,1)S(1)}, u32[]{:S(2)}, u32[]{:S(2)}) %collective-permute-start.4) | collective-permute-done | bytes 524320 | tf_op jit(solution)/shard_map/ppermute | solution.py:25
  101.1 3.6 %collective-permute-done.6.refs_5_.refs_7_ = bf16[128,2048]{1,0:T(8,128)(2,1)S(1)} collective-permute-done((bf16[128,2048]{1,0:T(8,128)(2,1)}, bf16[128,2048]{1,0:T(8,128)(2,1)S(1)}, u32[]{:S(2)}, u32[]{:S(2)}) %collective-permute-start.6) | collective-permute-done | bytes 524320 | tf_op jit(solution)/shard_map/ppermute | solution.py:25
  108.1 6.4 %dout.1 = (f32[1024,256]{1,0:T(8,128)}, bf16[1024,256]{1,0:T(8,128)(2,1)}) custom-call(bf16[128,2048]{1,0:T(8,128)(2,1)} %get-tuple-element.21.refs_4_.refs_2_.refs_0_, bf16[128,2048]{1,0:T(8,128)(2,1)} %copy-done.4, bf16[128,2048]{1,0:T(8,128)(2,1)} %copy-done.5, bf16[128,2048]{1,0:T(8,128)(2,1)} %collective-permute-done.2.refs_4_.refs_3_, ...), custom_call_target="tpu_custom_call" | custom-call | tf_op jit(solution)/shard_map/dout/pallas_call | solution.py:59
  116.4 6.3 %collective-permute-done.10.refs_9_ = bf16[256,1024]{1,0:T(8,128)(2,1)S(1)} collective-permute-done((bf16[256,1024]{1,0:T(8,128)(2,1)S(1)}, bf16[256,1024]{1,0:T(8,128)(2,1)S(1)}, u32[]{:S(2)}, u32[]{:S(2)}) %collective-permute-start.10) | collective-permute-done | bytes 524320 | tf_op jit(solution)/shard_map/ppermute | solution.py:25
  123.6 6.1 %out_terms.1 = (bf16[4,2,512,128]{3,2,1,0:T(8,128)(2,1)}, bf16[4,2,512,128]{3,2,1,0:T(8,128)(2,1)}) custom-call(bf16[128,2048]{1,0:T(8,128)(2,1)} %get-tuple-element.21.refs_4_.refs_2_.refs_0_, bf16[128,2048]{1,0:T(8,128)(2,1)} %copy-done.4, bf16[128,2048]{1,0:T(8,128)(2,1)} %copy-done.5, bf16[128,2048]{1,0:T(8,128)(2,1)} %collective-permute-done.2.refs_4_.refs_3_, ...), custom_call_target="tpu_custom_call" | custom-call | tf_op jit(solution)/shard_map/out_terms/pallas_call | solution.py:59
  129.7 3.4 %collective-permute-done.9 = bf16[1024,256]{1,0:T(8,128)(2,1)S(1)} collective-permute-done((bf16[1024,256]{1,0:T(8,128)(2,1)}, bf16[1024,256]{1,0:T(8,128)(2,1)S(1)}, u32[]{:S(2)}, u32[]{:S(2)}) %collective-permute-start.9) | collective-permute-done | bytes 524320 | tf_op jit(solution)/shard_map/ppermute | solution.py:25
  134.0 5.4 %attention_backward.2.refs_4_.refs_0_ = bf16[384,1024]{1,0:T(8,128)(2,1)} custom-call(s32[8]{0:T(128)} %stack.152.refs_0_, bf16[8,144,768]{2,1,0:T(8,128)(2,1)} %copy-done, bf16[2,1024,1024]{2,1,0:T(8,128)(2,1)} %get-tuple-element.22.refs_2_, bf16[1024,256]{1,0:T(8,128)(2,1)} %add_convert_fusion.3.refs_3_, bf16[4,2,512,128]{3,2,1,0:T(8,128)(2,1)} %get-tuple-element.29.refs_4_), custom_call_target="tpu_custom_call" | custom-call | tf_op jit(solution)/shard_map/attention_backward/pallas_call | solution.py:59
  139.5 5.4 %attention_backward.3.refs_1_ = bf16[384,1024]{1,0:T(8,128)(2,1)} custom-call(s32[8]{0:T(128)} %stack.152.refs_0_, bf16[8,144,768]{2,1,0:T(8,128)(2,1)} %copy-done, bf16[2,1024,1024]{2,1,0:T(8,128)(2,1)} %get-tuple-element.22.refs_2_, bf16[1024,256]{1,0:T(8,128)(2,1)} %add_convert_fusion.3.refs_3_, bf16[384,1024]{1,0:T(8,128)(2,1)} %attention_backward.2.refs_4_.refs_0_), custom_call_target="tpu_custom_call" | custom-call | tf_op jit(solution)/shard_map/attention_backward/pallas_call | solution.py:59
  149.1 5.0 %all-to-all-start.1 = ((bf16[4,2,512,128]{3,2,1,0:T(8,128)(2,1)}), bf16[4,2,512,128]{3,2,1,0:T(8,128)(2,1)S(1)}, u32[]{:S(2)}, u32[]{:S(2)}) async-start(bf16[4,2,512,128]{3,2,1,0:T(8,128)(2,1)} %add_convert_fusion.2), calls=%async_computation.1 | async-start | bytes 2097152 | tf_op jit(solution)/shard_map/all_to_all | solution.py:376
  154.4 13.6 %all-to-all-done.1 = bf16[4,2,512,128]{3,2,1,0:T(8,128)(2,1)S(1)} async-done(((bf16[4,2,512,128]{3,2,1,0:T(8,128)(2,1)}), bf16[4,2,512,128]{3,2,1,0:T(8,128)(2,1)S(1)}, u32[]{:S(2)}, u32[]{:S(2)}) %all-to-all-start.1) | async-done | bytes 1048608 | tf_op jit(solution)/shard_map/all_to_all | solution.py:376
  169.0 4.1 %collective-permute-done.12.refs_5_.refs_0_ = bf16[384,1024]{1,0:T(8,128)(2,1)S(1)} collective-permute-done((bf16[384,1024]{1,0:T(8,128)(2,1)S(1)}, bf16[384,1024]{1,0:T(8,128)(2,1)S(1)}, u32[]{:S(2)}, u32[]{:S(2)}) %collective-permute-start.12) | collective-permute-done | bytes 786464 | tf_op jit(solution)/shard_map/ppermute | solution.py:25
  174.1 7.3 %term_blocks.2 = (bf16[4,2,768,128]{3,2,1,0:T(8,128)(2,1)}, bf16[4,2,768,128]{3,2,1,0:T(8,128)(2,1)}) custom-call(bf16[384,1024]{1,0:T(8,128)(2,1)} %attention_backward.2.refs_4_.refs_0_, bf16[384,1024]{1,0:T(8,128)(2,1)} %attention_backward.3.refs_1_, bf16[1024,2048]{1,0:T(8,128)(2,1)} %all-gather.5.cloned.1.call-done.refs_2_, ...), custom_call_target="tpu_custom_call" | custom-call | tf_op jit(solution)/shard_map/term_blocks/pallas_call | solution.py:59
  181.4 3.6 %collective-permute-done.13 = bf16[4,2,768,128]{3,2,1,0:T(8,128)(2,1)S(1)} collective-permute-done((bf16[4,2,768,128]{3,2,1,0:T(8,128)(2,1)}, bf16[4,2,768,128]{3,2,1,0:T(8,128)(2,1)S(1)}, u32[]{:S(2)}, u32[]{:S(2)}) %collective-permute-start.13) | collective-permute-done | bytes 1572896 | tf_op jit(solution)/shard_map/ppermute | solution.py:25
  188.0 4.9 %all-to-all-start.2 = ((bf16[4,2,768,128]{3,2,1,0:T(8,128)(2,1)}), bf16[4,2,768,128]{3,2,1,0:T(8,128)(2,1)S(1)}, u32[]{:S(2)}, u32[]{:S(2)}) async-start(bf16[4,2,768,128]{3,2,1,0:T(8,128)(2,1)} %add_convert_fusion.1), calls=%async_computation.2 | async-start | bytes 3145728 | tf_op jit(solution)/shard_map/all_to_all | solution.py:376
  193.3 19.2 %all-to-all-done.2 = bf16[4,2,768,128]{3,2,1,0:T(8,128)(2,1)S(1)} async-done(((bf16[4,2,768,128]{3,2,1,0:T(8,128)(2,1)}), bf16[4,2,768,128]{3,2,1,0:T(8,128)(2,1)S(1)}, u32[]{:S(2)}, u32[]{:S(2)}) %all-to-all-start.2) | async-done | bytes 1572896 | tf_op jit(solution)/shard_map/all_to_all | solution.py:376
  214.5 7.3 %term_blocks.3 = (bf16[4,2,768,128]{3,2,1,0:T(8,128)(2,1)}, bf16[4,2,768,128]{3,2,1,0:T(8,128)(2,1)}) custom-call(bf16[384,1024]{1,0:T(8,128)(2,1)} %copy-done.11, bf16[384,1024]{1,0:T(8,128)(2,1)} %copy-done.15, bf16[1024,2048]{1,0:T(8,128)(2,1)} %all-gather.5.cloned.1.call-done.refs_2_, s32[5]{0:T(128)} %stack.158.refs_0_.refs_9_.refs_10_.refs_3_, ...), custom_call_target="tpu_custom_call" | custom-call | tf_op jit(solution)/shard_map/term_blocks/pallas_call | solution.py:59
  221.8 3.6 %collective-permute-done.19 = bf16[4,2,768,128]{3,2,1,0:T(8,128)(2,1)S(1)} collective-permute-done((bf16[4,2,768,128]{3,2,1,0:T(8,128)(2,1)}, bf16[4,2,768,128]{3,2,1,0:T(8,128)(2,1)S(1)}, u32[]{:S(2)}, u32[]{:S(2)}) %collective-permute-start.19) | collective-permute-done | bytes 1572896 | tf_op jit(solution)/shard_map/ppermute | solution.py:25
  225.4 3.0 %add_convert_fusion = bf16[4,2,768,128]{3,2,1,0:T(8,128)(2,1)} fusion(bf16[4,2,768,128]{3,2,1,0:T(8,128)(2,1)S(1)} %collective-permute-done.19, bf16[4,2,768,128]{3,2,1,0:T(8,128)(2,1)} %get-tuple-element.33), kind=kLoop, calls=%fused_computation | loop fusion | flops 3145728 | bytes 4718592 | tf_op jit(solution)/shard_map/convert_element_type | solution.py:243
  228.4 5.1 %all-to-all-start.3 = ((bf16[4,2,768,128]{3,2,1,0:T(8,128)(2,1)}), bf16[4,2,768,128]{3,2,1,0:T(8,128)(2,1)S(1)}, u32[]{:S(2)}, u32[]{:S(2)}) async-start(bf16[4,2,768,128]{3,2,1,0:T(8,128)(2,1)} %add_convert_fusion), calls=%async_computation.3 | async-start | bytes 3145728 | tf_op jit(solution)/shard_map/all_to_all | solution.py:376
  233.6 3.1 %collective-permute-start.23 = (bf16[256,128]{1,0:T(8,128)(2,1)S(1)}, bf16[256,128]{1,0:T(8,128)(2,1)S(1)}, u32[]{:S(2)}, u32[]{:S(2)}) collective-permute-start(bf16[256,128]{1,0:T(8,128)(2,1)S(1)} %get-tuple-element.47), channel_id=1, source_target_pairs={{0,68},{4,196},{64,4},{68,132},{128,64},{132,192},{192,0},{196,128... | collective-permute-start | bytes 196616 | tf_op jit(solution)/shard_map/ppermute | solution.py:35
  239.3 5.2 %collective-permute-start.20 = (bf16[256,128]{1,0:T(8,128)(2,1)S(1)}, bf16[256,128]{1,0:T(8,128)(2,1)S(1)}, u32[]{:S(2)}, u32[]{:S(2)}) collective-permute-start(bf16[256,128]{1,0:T(8,128)(2,1)S(1)} %get-tuple-element.44), channel_id=1, source_target_pairs={{0,0},{4,128},{64,64},{68,192},{128,4},{132,132},{192,68},{196,196... | collective-permute-start | bytes 196616 | tf_op jit(solution)/shard_map/ppermute | solution.py:35
  246.6 3.1 %collective-permute-start.16 = (bf16[768,128]{1,0:T(8,128)(2,1)S(1)}, bf16[768,128]{1,0:T(8,128)(2,1)S(1)}, u32[]{:S(2)}, u32[]{:S(2)}) collective-permute-start(bf16[768,128]{1,0:T(8,128)(2,1)S(1)} %get-tuple-element.40), channel_id=1, source_target_pairs={{0,0},{4,132},{64,64},{68,196},{1,1},{5,133},{65,65},{69,197},{2,2... | collective-permute-start | bytes 589832 | tf_op jit(solution)/shard_map/ppermute | solution.py:35
  250.4 3.0 %collective-permute-done.20 = bf16[256,128]{1,0:T(8,128)(2,1)S(1)} collective-permute-done((bf16[256,128]{1,0:T(8,128)(2,1)S(1)}, bf16[256,128]{1,0:T(8,128)(2,1)S(1)}, u32[]{:S(2)}, u32[]{:S(2)}) %collective-permute-start.20) | collective-permute-done | bytes 65568 | tf_op jit(solution)/shard_map/ppermute | solution.py:35
  262.3 14.3 %collective-permute-start.26 = (bf16[768,128]{1,0:T(8,128)(2,1)S(1)}, bf16[768,128]{1,0:T(8,128)(2,1)S(1)}, u32[]{:S(2)}, u32[]{:S(2)}) collective-permute-start(bf16[768,128]{1,0:T(8,128)(2,1)S(1)} %get-tuple-element.38), channel_id=1, source_target_pairs={{0,4},{4,128},{64,68},{68,192},{1,5},{5,129},{65,69},{69,193},{2,6... | collective-permute-start | bytes 589832 | tf_op jit(solution)/shard_map/ppermute | solution.py:35
  279.8 7.4 %collective-permute-done.27.refs_7_ = bf16[768,128]{1,0:T(8,128)(2,1)S(1)} collective-permute-done((bf16[768,128]{1,0:T(8,128)(2,1)S(1)}, bf16[768,128]{1,0:T(8,128)(2,1)S(1)}, u32[]{:S(2)}, u32[]{:S(2)}) %collective-permute-start.27) | collective-permute-done | bytes 196640 | tf_op jit(solution)/shard_map/ppermute | solution.py:35
  (123 shorter events, 62.3 us)
Async XLA Ops:
  7.2 100.9 %all-gather.3.cloned.1.call-start = ((), (), s32[]{:S(2)}) async-start(), calls=%async_computation.4 | async-start | bytes 2162688 | tf_op jit(solution)/shard_map/all_gather | solution.py:264
  7.2 9.4 %collective-permute-start.7 = (bf16[256,128]{1,0:T(8,128)(2,1)}, bf16[256,128]{1,0:T(8,128)(2,1)S(1)}, u32[]{:S(2)}, u32[]{:S(2)}) collective-permute-start(bf16[256,128]{1,0:T(8,128)(2,1)} %param.14), channel_id=1, source_target_pairs={{0,0},{4,128},{64,64},{68,192},{128,4},{132,132},{192,68},{196,196... | collective-permute-start | bytes 196616 | tf_op jit(solution)/shard_map/ppermute | solution.py:35
  25.3 49.3 %all-to-all-start = ((bf16[8,144,768]{2,1,0:T(8,128)(2,1)}), bf16[8,144,768]{2,1,0:T(8,128)(2,1)S(1)}, u32[]{:S(2)}, u32[]{:S(2)}) async-start(bf16[8,144,768]{2,1,0:T(8,128)(2,1)} %pack.1), calls=%async_computation | async-start | bytes 3538944 | tf_op jit(solution)/shard_map/all_to_all | solution.py:304
  31.1 142.0 %all-gather.5.cloned.1.call-start = ((), (), s32[]{:S(2)}) async-start(), calls=%async_computation.5 | async-start | bytes 5242880 | tf_op jit(solution)/shard_map/all_gather | solution.py:329
  31.2 30.9 %collective-permute-start = (bf16[128,2048]{1,0:T(8,128)(2,1)S(1)}, bf16[128,2048]{1,0:T(8,128)(2,1)S(1)}, u32[]{:S(2)}, u32[]{:S(2)}) collective-permute-start(bf16[128,2048]{1,0:T(8,128)(2,1)S(1)} %copy-done.1), channel_id=1, source_target_pairs={{1,0},{2,1},{3,2},{0,3},{5,4},{6,5},{7,6},{4,7},{9,8},{10,9},{11,1... | collective-permute-start | bytes 1572872 | tf_op jit(solution)/shard_map/ppermute | solution.py:25
  33.9 32.2 %collective-permute-start.1 = (bf16[128,2048]{1,0:T(8,128)(2,1)S(1)}, bf16[128,2048]{1,0:T(8,128)(2,1)S(1)}, u32[]{:S(2)}, u32[]{:S(2)}) collective-permute-start(bf16[128,2048]{1,0:T(8,128)(2,1)S(1)} %copy-done.1), channel_id=1, source_target_pairs={{2,0},{3,1},{0,2},{1,3},{6,4},{7,5},{4,6},{5,7},{10,8},{11,9},{8,1... | collective-permute-start | bytes 1572872 | tf_op jit(solution)/shard_map/ppermute | solution.py:25
  34.8 39.8 %collective-permute-start.2 = (bf16[128,2048]{1,0:T(8,128)(2,1)S(1)}, bf16[128,2048]{1,0:T(8,128)(2,1)}, u32[]{:S(2)}, u32[]{:S(2)}) collective-permute-start(bf16[128,2048]{1,0:T(8,128)(2,1)S(1)} %copy-done.1), channel_id=1, source_target_pairs={{3,0},{0,1},{1,2},{2,3},{7,4},{4,5},{5,6},{6,7},{11,8},{8,9},{9,10... | collective-permute-start | bytes 1572872 | tf_op jit(solution)/shard_map/ppermute | solution.py:25
  35.6 38.9 %collective-permute-start.3 = (bf16[128,2048]{1,0:T(8,128)(2,1)}, bf16[128,2048]{1,0:T(8,128)(2,1)}, u32[]{:S(2)}, u32[]{:S(2)}) collective-permute-start(bf16[128,2048]{1,0:T(8,128)(2,1)} %get-tuple-element.23), channel_id=1, source_target_pairs={{4,0},{0,4},{5,1},{1,5},{6,2},{2,6},{7,3},{3,7},{12,8},{8,12},{13,... | collective-permute-start | bytes 1572872 | tf_op jit(solution)/shard_map/ppermute | solution.py:25
  39.4 51.0 %collective-permute-start.8 = (bf16[128,2048]{1,0:T(8,128)(2,1)}, bf16[128,2048]{1,0:T(8,128)(2,1)}, u32[]{:S(2)}, u32[]{:S(2)}) collective-permute-start(bf16[128,2048]{1,0:T(8,128)(2,1)} %get-tuple-element.25), channel_id=1, source_target_pairs={{4,0},{0,4},{5,1},{1,5},{6,2},{2,6},{7,3},{3,7},{12,8},{8,12},{13,... | collective-permute-start | bytes 1572872 | tf_op jit(solution)/shard_map/ppermute | solution.py:25
  75.9 25.2 %collective-permute-start.4 = (bf16[128,2048]{1,0:T(8,128)(2,1)}, bf16[128,2048]{1,0:T(8,128)(2,1)S(1)}, u32[]{:S(2)}, u32[]{:S(2)}) collective-permute-start(bf16[128,2048]{1,0:T(8,128)(2,1)} %gate.3.refs_4_), channel_id=1, source_target_pairs={{1,0},{2,1},{3,2},{0,3},{5,4},{6,5},{7,6},{4,7},{9,8},{10,9},{11,1... | collective-permute-start | bytes 1572872 | tf_op jit(solution)/shard_map/ppermute | solution.py:25
  78.0 23.1 %collective-permute-start.5 = (bf16[128,2048]{1,0:T(8,128)(2,1)}, bf16[128,2048]{1,0:T(8,128)(2,1)S(1)}, u32[]{:S(2)}, u32[]{:S(2)}) collective-permute-start(bf16[128,2048]{1,0:T(8,128)(2,1)} %gate.3.refs_4_), channel_id=1, source_target_pairs={{2,0},{3,1},{0,2},{1,3},{6,4},{7,5},{4,6},{5,7},{10,8},{11,9},{8,1... | collective-permute-start | bytes 1572872 | tf_op jit(solution)/shard_map/ppermute | solution.py:25
  79.5 25.2 %collective-permute-start.6 = (bf16[128,2048]{1,0:T(8,128)(2,1)}, bf16[128,2048]{1,0:T(8,128)(2,1)S(1)}, u32[]{:S(2)}, u32[]{:S(2)}) collective-permute-start(bf16[128,2048]{1,0:T(8,128)(2,1)} %gate.3.refs_4_), channel_id=1, source_target_pairs={{3,0},{0,1},{1,2},{2,3},{7,4},{4,5},{5,6},{6,7},{11,8},{8,9},{9,10... | collective-permute-start | bytes 1572872 | tf_op jit(solution)/shard_map/ppermute | solution.py:25
  107.7 15.1 %collective-permute-start.10 = (bf16[256,1024]{1,0:T(8,128)(2,1)S(1)}, bf16[256,1024]{1,0:T(8,128)(2,1)S(1)}, u32[]{:S(2)}, u32[]{:S(2)}) collective-permute-start(bf16[256,1024]{1,0:T(8,128)(2,1)S(1)} %copy-done.13), channel_id=1, source_target_pairs={{4,0},{0,4},{5,1},{1,5},{6,2},{2,6},{7,3},{3,7},{12,8},{8,12},{13,... | collective-permute-start | bytes 1572872 | tf_op jit(solution)/shard_map/ppermute | solution.py:25
  114.5 18.6 %collective-permute-start.9 = (bf16[1024,256]{1,0:T(8,128)(2,1)}, bf16[1024,256]{1,0:T(8,128)(2,1)S(1)}, u32[]{:S(2)}, u32[]{:S(2)}) collective-permute-start(bf16[1024,256]{1,0:T(8,128)(2,1)} %get-tuple-element.28.refs_11_), channel_id=1, source_target_pairs={{4,0},{0,4},{5,1},{1,5},{6,2},{2,6},{7,3},{3,7},{12,8},{8,12},{13,... | collective-permute-start | bytes 1572872 | tf_op jit(solution)/shard_map/ppermute | solution.py:25
  149.1 19.0 %all-to-all-start.1 = ((bf16[4,2,512,128]{3,2,1,0:T(8,128)(2,1)}), bf16[4,2,512,128]{3,2,1,0:T(8,128)(2,1)S(1)}, u32[]{:S(2)}, u32[]{:S(2)}) async-start(bf16[4,2,512,128]{3,2,1,0:T(8,128)(2,1)} %add_convert_fusion.2), calls=%async_computation.1 | async-start | bytes 2097152 | tf_op jit(solution)/shard_map/all_to_all | solution.py:376
  154.1 19.0 %collective-permute-start.12 = (bf16[384,1024]{1,0:T(8,128)(2,1)S(1)}, bf16[384,1024]{1,0:T(8,128)(2,1)S(1)}, u32[]{:S(2)}, u32[]{:S(2)}) collective-permute-start(bf16[384,1024]{1,0:T(8,128)(2,1)S(1)} %copy-done.2), channel_id=1, source_target_pairs={{4,0},{0,4},{5,1},{1,5},{6,2},{2,6},{7,3},{3,7},{12,8},{8,12},{13,... | collective-permute-start | bytes 2359304 | tf_op jit(solution)/shard_map/ppermute | solution.py:25
  188.0 24.5 %all-to-all-start.2 = ((bf16[4,2,768,128]{3,2,1,0:T(8,128)(2,1)}), bf16[4,2,768,128]{3,2,1,0:T(8,128)(2,1)S(1)}, u32[]{:S(2)}, u32[]{:S(2)}) async-start(bf16[4,2,768,128]{3,2,1,0:T(8,128)(2,1)} %add_convert_fusion.1), calls=%async_computation.2 | async-start | bytes 3145728 | tf_op jit(solution)/shard_map/all_to_all | solution.py:376
  192.9 20.6 %collective-permute-start.18 = (bf16[384,1024]{1,0:T(8,128)(2,1)S(1)}, bf16[384,1024]{1,0:T(8,128)(2,1)S(1)}, u32[]{:S(2)}, u32[]{:S(2)}) collective-permute-start(bf16[384,1024]{1,0:T(8,128)(2,1)S(1)} %copy-done.3), channel_id=1, source_target_pairs={{4,0},{0,4},{5,1},{1,5},{6,2},{2,6},{7,3},{3,7},{12,8},{8,12},{13,... | collective-permute-start | bytes 2359304 | tf_op jit(solution)/shard_map/ppermute | solution.py:25
  221.8 3.6 %collective-permute-start.19 = (bf16[4,2,768,128]{3,2,1,0:T(8,128)(2,1)}, bf16[4,2,768,128]{3,2,1,0:T(8,128)(2,1)S(1)}, u32[]{:S(2)}, u32[]{:S(2)}) collective-permute-start(bf16[4,2,768,128]{3,2,1,0:T(8,128)(2,1)} %get-tuple-element.34), channel_id=1, source_target_pairs={{8,0},{0,8},{9,1},{1,9},{10,2},{2,10},{11,3},{3,11},{12,4},{4,12},... | collective-permute-start | bytes 4718600 | tf_op jit(solution)/shard_map/ppermute | solution.py:25
  228.4 25.7 %all-to-all-start.3 = ((bf16[4,2,768,128]{3,2,1,0:T(8,128)(2,1)}), bf16[4,2,768,128]{3,2,1,0:T(8,128)(2,1)S(1)}, u32[]{:S(2)}, u32[]{:S(2)}) async-start(bf16[4,2,768,128]{3,2,1,0:T(8,128)(2,1)} %add_convert_fusion), calls=%async_computation.3 | async-start | bytes 3145728 | tf_op jit(solution)/shard_map/all_to_all | solution.py:376
  233.6 12.3 %collective-permute-start.23 = (bf16[256,128]{1,0:T(8,128)(2,1)S(1)}, bf16[256,128]{1,0:T(8,128)(2,1)S(1)}, u32[]{:S(2)}, u32[]{:S(2)}) collective-permute-start(bf16[256,128]{1,0:T(8,128)(2,1)S(1)} %get-tuple-element.47), channel_id=1, source_target_pairs={{0,68},{4,196},{64,4},{68,132},{128,64},{132,192},{192,0},{196,128... | collective-permute-start | bytes 196616 | tf_op jit(solution)/shard_map/ppermute | solution.py:35
  236.7 9.9 %collective-permute-start.22 = (bf16[256,128]{1,0:T(8,128)(2,1)S(1)}, bf16[256,128]{1,0:T(8,128)(2,1)S(1)}, u32[]{:S(2)}, u32[]{:S(2)}) collective-permute-start(bf16[256,128]{1,0:T(8,128)(2,1)S(1)} %get-tuple-element.46), channel_id=1, source_target_pairs={{0,64},{4,192},{64,0},{68,128},{128,68},{132,196},{192,4},{196,132... | collective-permute-start | bytes 196616 | tf_op jit(solution)/shard_map/ppermute | solution.py:35
  236.7 13.0 %collective-permute-start.21 = (bf16[256,128]{1,0:T(8,128)(2,1)S(1)}, bf16[256,128]{1,0:T(8,128)(2,1)S(1)}, u32[]{:S(2)}, u32[]{:S(2)}) collective-permute-start(bf16[256,128]{1,0:T(8,128)(2,1)S(1)} %get-tuple-element.45), channel_id=1, source_target_pairs={{0,4},{4,132},{64,68},{68,196},{128,0},{132,128},{192,64},{196,192... | collective-permute-start | bytes 196616 | tf_op jit(solution)/shard_map/ppermute | solution.py:35
  239.3 14.2 %collective-permute-start.20 = (bf16[256,128]{1,0:T(8,128)(2,1)S(1)}, bf16[256,128]{1,0:T(8,128)(2,1)S(1)}, u32[]{:S(2)}, u32[]{:S(2)}) collective-permute-start(bf16[256,128]{1,0:T(8,128)(2,1)S(1)} %get-tuple-element.44), channel_id=1, source_target_pairs={{0,0},{4,128},{64,64},{68,192},{128,4},{132,132},{192,68},{196,196... | collective-permute-start | bytes 196616 | tf_op jit(solution)/shard_map/ppermute | solution.py:35
  244.6 10.7 %collective-permute-start.14 = (bf16[768,128]{1,0:T(8,128)(2,1)S(1)}, bf16[768,128]{1,0:T(8,128)(2,1)S(1)}, u32[]{:S(2)}, u32[]{:S(2)}) collective-permute-start(bf16[768,128]{1,0:T(8,128)(2,1)S(1)} %get-tuple-element.41), channel_id=1, source_target_pairs={{0,64},{4,196},{64,0},{68,132},{1,65},{5,197},{65,1},{69,133},{2,6... | collective-permute-start | bytes 589832 | tf_op jit(solution)/shard_map/ppermute | solution.py:35
  245.9 9.4 %collective-permute-start.15 = (bf16[768,128]{1,0:T(8,128)(2,1)S(1)}, bf16[768,128]{1,0:T(8,128)(2,1)S(1)}, u32[]{:S(2)}, u32[]{:S(2)}) collective-permute-start(bf16[768,128]{1,0:T(8,128)(2,1)S(1)} %get-tuple-element.41), channel_id=1, source_target_pairs={{128,64},{132,196},{192,0},{196,132},{129,65},{133,197},{193,1},{1... | collective-permute-start | bytes 589832 | tf_op jit(solution)/shard_map/ppermute | solution.py:35
  246.6 9.6 %collective-permute-start.16 = (bf16[768,128]{1,0:T(8,128)(2,1)S(1)}, bf16[768,128]{1,0:T(8,128)(2,1)S(1)}, u32[]{:S(2)}, u32[]{:S(2)}) collective-permute-start(bf16[768,128]{1,0:T(8,128)(2,1)S(1)} %get-tuple-element.40), channel_id=1, source_target_pairs={{0,0},{4,132},{64,64},{68,196},{1,1},{5,133},{65,65},{69,197},{2,2... | collective-permute-start | bytes 589832 | tf_op jit(solution)/shard_map/ppermute | solution.py:35
  249.8 6.5 %collective-permute-start.17 = (bf16[768,128]{1,0:T(8,128)(2,1)S(1)}, bf16[768,128]{1,0:T(8,128)(2,1)S(1)}, u32[]{:S(2)}, u32[]{:S(2)}) collective-permute-start(bf16[768,128]{1,0:T(8,128)(2,1)S(1)} %get-tuple-element.40), channel_id=1, source_target_pairs={{128,0},{132,132},{192,64},{196,196},{129,1},{133,133},{193,65},{1... | collective-permute-start | bytes 589832 | tf_op jit(solution)/shard_map/ppermute | solution.py:35
  258.6 19.3 %collective-permute-start.24 = (bf16[768,128]{1,0:T(8,128)(2,1)S(1)}, bf16[768,128]{1,0:T(8,128)(2,1)S(1)}, u32[]{:S(2)}, u32[]{:S(2)}) collective-permute-start(bf16[768,128]{1,0:T(8,128)(2,1)S(1)} %get-tuple-element.39), channel_id=1, source_target_pairs={{0,68},{4,192},{64,4},{68,128},{1,69},{5,193},{65,5},{69,129},{2,7... | collective-permute-start | bytes 589832 | tf_op jit(solution)/shard_map/ppermute | solution.py:35
  261.0 17.0 %collective-permute-start.25 = (bf16[768,128]{1,0:T(8,128)(2,1)S(1)}, bf16[768,128]{1,0:T(8,128)(2,1)S(1)}, u32[]{:S(2)}, u32[]{:S(2)}) collective-permute-start(bf16[768,128]{1,0:T(8,128)(2,1)S(1)} %get-tuple-element.39), channel_id=1, source_target_pairs={{128,68},{132,192},{192,4},{196,128},{129,69},{133,193},{193,5},{1... | collective-permute-start | bytes 589832 | tf_op jit(solution)/shard_map/ppermute | solution.py:35
  262.3 17.5 %collective-permute-start.26 = (bf16[768,128]{1,0:T(8,128)(2,1)S(1)}, bf16[768,128]{1,0:T(8,128)(2,1)S(1)}, u32[]{:S(2)}, u32[]{:S(2)}) collective-permute-start(bf16[768,128]{1,0:T(8,128)(2,1)S(1)} %get-tuple-element.38), channel_id=1, source_target_pairs={{0,4},{4,128},{64,68},{68,192},{1,5},{5,129},{65,69},{69,193},{2,6... | collective-permute-start | bytes 589832 | tf_op jit(solution)/shard_map/ppermute | solution.py:35
  276.6 10.6 %collective-permute-start.27 = (bf16[768,128]{1,0:T(8,128)(2,1)S(1)}, bf16[768,128]{1,0:T(8,128)(2,1)S(1)}, u32[]{:S(2)}, u32[]{:S(2)}) collective-permute-start(bf16[768,128]{1,0:T(8,128)(2,1)S(1)} %get-tuple-element.38), channel_id=1, source_target_pairs={{128,4},{132,128},{192,68},{196,192},{129,5},{133,129},{193,69},{1... | collective-permute-start | bytes 589832 | tf_op jit(solution)/shard_map/ppermute | solution.py:35
  (28 other events, 130.8 us)
Sparse Core Ops, SparseCore 0:
  17.4 59.4 all-gather.2
  107.9 50.0 all-gather.4
where the time goes:
time: 298 us; the launch traced here: 297 us
  waiting for transfers between devices  121 us (41%)
  starting transfers between devices  75.9 us (25%)
  Pallas kernels  60.9 us (20%)
  between operations  15 us (5%)
  other arithmetic  12.7 us (4%)
  local copies, waits for them, and re-layouts  11.2 us (4%)
    ppermute x15, waiting for transfers between devices, recv(): return lax.ppermute(block, axis, [((i + offset) % n, i) for i in range(n)])  71.9 us
    pallas_call x12, Pallas kernels, call(): pl.pallas_call(body, grid=grid, out_shape=outs, in_specs=[whole(s, a) for...  60.9 us
    ppermute x13, starting transfers between devices, send_zz(): return lax.ppermute(block, ('h', 'l'), pairs)  41.9 us
    all_to_all x3, waiting for transfers between devices, y_sum(): lax.all_to_all(blocks, 'y', split_axis=0, concat_axis=0, tiled=True)  32.9 us
    ppermute x13, waiting for transfers between devices, send_zz(): return lax.ppermute(block, ('h', 'l'), pairs)  16.6 us
    all_to_all x3, starting transfers between devices, y_sum(): lax.all_to_all(blocks, 'y', split_axis=0, concat_axis=0, tiled=True)  15.1 us
    ppermute x15, starting transfers between devices, recv(): return lax.ppermute(block, axis, [((i + offset) % n, i) for i in range(n)])  13 us
    unnamed x52, local copies, waits for them, and re-layouts  7.41 us
  transfers between devices with their start and end apart: 34, of which 18 were waited for; matrix products, arithmetic and copies ran while one was open for 3% of the time, Pallas kernels for 15%

commit v1 on v0

--- a/solution.py
+++ b/solution.py
@@ -208,23 +208,22 @@
 
 
 def term_blocks(lhs, slab, place, flip, deps):
-    n, m = len(lhs), sum(a.shape[0] for a in lhs)
-
-    def kernel(*refs):
-        slab_ref, place_ref, send_ref, keep_ref = refs[n:]
-        left = jnp.concatenate([by_x(r, place_ref[4], flip) for r in refs[:n]], axis=0)
+    m = lhs.shape[0]
+
+    def kernel(lhs_ref, slab_ref, place_ref, send_ref, keep_ref):
+        left = by_x(lhs_ref, place_ref[4], flip)
         for tile in range(8):
             cols = slice(tile * 256, (tile + 1) * 256)
             term = dot(left, slab_ref[:, cols], ((1,), (0,))).astype(BF16)
             out = send_ref if tile % 4 < 2 else keep_ref
-            out[(tile % 2) * 2, tile // 4] = term[:, :128]
-            out[(tile % 2) * 2 + 1, tile // 4] = term[:, 128:]
+            out[tile % 2 * 2, tile // 4] = term[:, :128]
+            out[tile % 2 * 2 + 1, tile // 4] = term[:, 128:]
 
     return call(
         kernel,
         "term_blocks",
-        list(lhs) + [slab, place],
-        [VMEM] * (n + 1) + [SMEM],
+        [lhs, slab, place],
+        [VMEM, VMEM, SMEM],
         (shape(4, 2, m, 128), shape(4, 2, m, 128)),
         (VMEM, VMEM),
         deps=deps,
@@ -324,7 +323,7 @@
         [VMEM, VMEM],
         shape(2 * TOK, HALF),
         VMEM,
-        deps=[attended] + scaled[5:],
+        deps=[attended_pair, out_rows] + scaled[5:],
     )
     slab = lax.all_gather(layer, "x", axis=0, tiled=True)
     dout_keep, dout_send = call(
@@ -347,27 +346,23 @@
         (VMEM, VMEM),
         deps=[dout_send],
     )
-
-    def backward(head, deps):
-        return call(
-            backward_kernel,
-            "attention_backward",
-            [idx, packed, probs, dout],
-            [
-                SMEM,
-                pl.BlockSpec((8, TOK + 16, 384), lambda i: (0, 0, head)),
-                pl.BlockSpec((1, 1024, 1024), lambda i: (head, 0, 0)),
-                pl.BlockSpec((1024, HEAD), lambda i: (0, head)),
-            ],
-            shape(384, 1024),
-            pl.BlockSpec((384, 1024), lambda i: (0, 0)),
-            deps=deps,
-            scratch=[pltpu.VMEM((HEAD, 1024), F32), pltpu.VMEM((HEAD, 1024), F32)],
-        )
-
-    terms_t = [backward(0, [out_keep])]
-    terms_t.append(backward(1, [terms_t[0]]))
-    terms_pair = [recv(t, "l", 1) for t in terms_t]
+    terms_t = call(
+        backward_kernel,
+        "attention_backward",
+        [idx, packed, probs, dout],
+        [
+            SMEM,
+            pl.BlockSpec((8, TOK + 16, 384), lambda i: (0, 0, i)),
+            pl.BlockSpec((1, 1024, 1024), lambda i: (i, 0, 0)),
+            pl.BlockSpec((1024, HEAD), lambda i: (0, i)),
+        ],
+        shape(768, 1024),
+        pl.BlockSpec((384, 1024), lambda i: (i, 0)),
+        deps=[out_keep],
+        grid=(2,),
+        scratch=[pltpu.VMEM((HEAD, 1024), F32), pltpu.VMEM((HEAD, 1024), F32)],
+    )
+    terms_pair = recv(terms_t, "l", 1)
 
     def core_sum(send, keep):
         return add_low(keep, recv(send, "c", 1))
@@ -376,8 +371,22 @@
         arrived = lax.all_to_all(blocks, "y", split_axis=0, concat_axis=0, tiled=True)
         return jnp.sum(arrived.astype(F32), axis=0).astype(BF16)
 
-    out_blocks = core_sum(gate(out_send, [terms_t[1]]), out_keep)
-    out_part = y_sum(out_blocks)
+    def y_permuted(blocks):
+        part = 0.0
+        for dy in (2, 1, 3, 0):
+            block = lax.dynamic_index_in_dim(blocks, (y + dy) % 4, 0, keepdims=False)
+            part = part + (recv(block, "y", 4 - dy) if dy else block).astype(F32)
+        return part.astype(BF16)
+
+    out_part = y_permuted(core_sum(gate(out_send, [terms_t]), out_keep))
+
+    send, keep = term_blocks(terms_t, slab, place, False, [out_part])
+    part = y_permuted(core_sum(send, keep))
+    full = []
+    for i, a in enumerate((1, 0)):
+        for s in range(2):
+            full.append(send_zz(part[i], lambda h1, h0, l: (l, h0 ^ a, l), s))
+
     grad_out = 0.0
     for a in range(2):
         for b in range(2):
@@ -385,14 +394,7 @@
             chosen = send_zz(chosen, lambda h1, h0, l: (l, h0 ^ a, h1 ^ b))
             grad_out = grad_out + chosen.astype(F32)
 
-    deps = [out_part, terms_pair[0]]
-    blocks = core_sum(*term_blocks(terms_t, slab, place, False, deps))
-    part = y_sum(blocks)
-    full = []
-    for i, a in enumerate((1, 0)):
-        for s in range(2):
-            full.append(send_zz(part[i], lambda h1, h0, l: (l, h0 ^ a, l), s))
-    blocks = core_sum(*term_blocks(terms_pair, slab, place, True, [part]))
+    blocks = gate(core_sum(*term_blocks(terms_pair, slab, place, True, [keep])), [part])
     part = gate(y_sum(blocks), [grad_out] + full)
     for i, a in enumerate((1, 0)):
         for s in range(2):

time: 298 us -> 275 us (0.923)
  waiting for transfers between devices: 121 us -> 102 us
  other arithmetic: 12.7 us -> 9.59 us
    all_to_all x3 -> x1, waiting for transfers between devices: 32.9 us -> 0.01 us  [y_sum(): lax.all_to_all(blocks, 'y', split_axis=0, concat_axis=0, tiled=True)]
    ppermute x15 -> x20, waiting for transfers between devices: 71.9 us -> 85.9 us  [recv(): return lax.ppermute(block, axis, [((i + offset) % n, i) for i in range(n)])]
    ppermute x15 -> x20, starting transfers between devices: 13 us -> 23.6 us  [recv(): return lax.ppermute(block, axis, [((i + offset) % n, i) for i in range(n)])]
    all_to_all x3 -> x1, starting transfers between devices: 15.1 us -> 6.95 us  [y_sum(): lax.all_to_all(blocks, 'y', split_axis=0, concat_axis=0, tiled=True)]
    convert_element_type x3, other arithmetic: 7.27 us -> 3.47 us  [add_low(): return (a.astype(F32) + b.astype(F32)).astype(BF16)]
    pallas_call x12 -> x11, Pallas kernels: 60.9 us -> 58.2 us  [call(): pl.pallas_call(body, grid=grid, out_shape=outs, in_specs=[whole(s, a) for...]
    unnamed x52 -> x50, local copies, waits for them, and re-layouts: 7.41 us -> 7.21 us
  transfers between devices with their start and end apart: 34 -> 37, of which waited for: 18 -> 19; matrix products, arithmetic and copies ran while one was open for 3% -> 4% of each run, Pallas kernels for 15% -> 19%
where the time goes in v1:
time: 275 us; the launch traced here: 274 us
  waiting for transfers between devices  102 us (37%)
  starting transfers between devices  77.9 us (28%)
  Pallas kernels  58.2 us (21%)
  between operations  15.1 us (5%)
  local copies, waits for them, and re-layouts  11.3 us (4%)
  other arithmetic  9.59 us (3%)
    ppermute x20, waiting for transfers between devices, recv(): return lax.ppermute(block, axis, [((i + offset) % n, i) for i in range(n)])  85.9 us
    pallas_call x11, Pallas kernels, call(): pl.pallas_call(body, grid=grid, out_shape=outs, in_specs=[whole(s, a) for...  58.2 us
    ppermute x13, starting transfers between devices, send_zz(): return lax.ppermute(block, ('h', 'l'), pairs)  41.5 us
    ppermute x20, starting transfers between devices, recv(): return lax.ppermute(block, axis, [((i + offset) % n, i) for i in range(n)])  23.6 us
    ppermute x13, waiting for transfers between devices, send_zz(): return lax.ppermute(block, ('h', 'l'), pairs)  16.3 us
    unnamed x50, local copies, waits for them, and re-layouts  7.21 us
    all_to_all x1, starting transfers between devices, y_sum(): lax.all_to_all(blocks, 'y', split_axis=0, concat_axis=0, tiled=True)  6.95 us
    all_to_all x1, starting transfers between devices, shards(): lax.all_to_all(to_heads, SEQ, split_axis=0, concat_axis=0, tiled=True)  5.89 us
  transfers between devices with their start and end apart: 37, of which 19 were waited for; matrix products, arithmetic and copies ran while one was open for 4% of the time, Pallas kernels for 19%

profile of v1, /device:TPU:104, one launch (start us, length us, event | category | flops | bytes accessed | tf_op | source)
XLA Modules:
  0.0 274.3 jit_solution(12056646241660440722)
XLA Ops:
  7.2 5.9 %collective-permute-start.7 = (bf16[256,128]{1,0:T(8,128)(2,1)}, bf16[256,128]{1,0:T(8,128)(2,1)S(1)}, u32[]{:S(2)}, u32[]{:S(2)}) collective-permute-start(bf16[256,128]{1,0:T(8,128)(2,1)} %param.14), channel_id=1, source_target_pairs={{0,0},{4,128},{64,64},{68,192},{128,4},{132,132},{192,68},{196,196... | collective-permute-start | bytes 196616 | tf_op jit(solution)/shard_map/ppermute | solution.py:35
  13.2 3.4 %collective-permute-done.7 = bf16[256,128]{1,0:T(8,128)(2,1)S(1)} collective-permute-done((bf16[256,128]{1,0:T(8,128)(2,1)}, bf16[256,128]{1,0:T(8,128)(2,1)S(1)}, u32[]{:S(2)}, u32[]{:S(2)}) %collective-permute-start.7) | collective-permute-done | bytes 65568 | tf_op jit(solution)/shard_map/ppermute | solution.py:35
  20.0 2.5 scale.1
  22.5 2.9 %pack.1 = bf16[8,144,768]{2,1,0:T(8,128)(2,1)} custom-call(bf16[128,2048]{1,0:T(8,128)(2,1)} %refs_0_.1, bf16[128,2048]{1,0:T(8,128)(2,1)} %refs_1_.4, bf16[128,2048]{1,0:T(8,128)(2,1)} %refs_2_.1, s32[1,128]{1,0:T(1,128)} %refs_3_.1, bf16[128,2048]{1,0:T(8,128)(2,1)} %get-tuple-element.21.refs_4_.refs_2_.refs_0_), custom_call_target="tpu_custom_call" | custom-call | tf_op jit(solution)/shard_map/pack/pallas_call | solution.py:59
  25.4 5.9 %all-to-all-start = ((bf16[8,144,768]{2,1,0:T(8,128)(2,1)}), bf16[8,144,768]{2,1,0:T(8,128)(2,1)S(1)}, u32[]{:S(2)}, u32[]{:S(2)}) async-start(bf16[8,144,768]{2,1,0:T(8,128)(2,1)} %pack.1), calls=%async_computation | async-start | bytes 3538944 | tf_op jit(solution)/shard_map/all_to_all | solution.py:303
  31.3 2.8 %collective-permute-start = (bf16[128,2048]{1,0:T(8,128)(2,1)S(1)}, bf16[128,2048]{1,0:T(8,128)(2,1)S(1)}, u32[]{:S(2)}, u32[]{:S(2)}) collective-permute-start(bf16[128,2048]{1,0:T(8,128)(2,1)S(1)} %copy-done.2), channel_id=1, source_target_pairs={{1,0},{2,1},{3,2},{0,3},{5,4},{6,5},{7,6},{4,7},{9,8},{10,9},{11,1... | collective-permute-start | bytes 1572872 | tf_op jit(solution)/shard_map/ppermute | solution.py:25
  37.0 2.5 reorder.1
  41.7 20.5 %collective-permute-done.refs_2_.refs_1_ = bf16[128,2048]{1,0:T(8,128)(2,1)S(1)} collective-permute-done((bf16[128,2048]{1,0:T(8,128)(2,1)S(1)}, bf16[128,2048]{1,0:T(8,128)(2,1)S(1)}, u32[]{:S(2)}, u32[]{:S(2)}) %collective-permute-start) | collective-permute-done | bytes 524320 | tf_op jit(solution)/shard_map/ppermute | solution.py:25
  62.2 4.0 %collective-permute-done.1.refs_3_.refs_2_ = bf16[128,2048]{1,0:T(8,128)(2,1)S(1)} collective-permute-done((bf16[128,2048]{1,0:T(8,128)(2,1)S(1)}, bf16[128,2048]{1,0:T(8,128)(2,1)S(1)}, u32[]{:S(2)}, u32[]{:S(2)}) %collective-permute-start.1) | collective-permute-done | bytes 524320 | tf_op jit(solution)/shard_map/ppermute | solution.py:25
  66.2 8.5 %collective-permute-done.2.refs_4_.refs_3_ = bf16[128,2048]{1,0:T(8,128)(2,1)} collective-permute-done((bf16[128,2048]{1,0:T(8,128)(2,1)S(1)}, bf16[128,2048]{1,0:T(8,128)(2,1)}, u32[]{:S(2)}, u32[]{:S(2)}) %collective-permute-start.2) | collective-permute-done | bytes 524320 | tf_op jit(solution)/shard_map/ppermute | solution.py:25
  79.6 10.2 %attention_forward.1 = (bf16[256,1024]{1,0:T(8,128)(2,1)}, bf16[2,1024,1024]{2,1,0:T(8,128)(2,1)}) custom-call(s32[8]{0:T(128)} %stack.152.refs_0_, bf16[8,144,768]{2,1,0:T(8,128)(2,1)} %copy-done), custom_call_target="tpu_custom_call" | custom-call | tf_op jit(solution)/shard_map/attention_forward/pallas_call | solution.py:59
  91.8 9.3 %collective-permute-done.4.refs_4_.refs_5_ = bf16[128,2048]{1,0:T(8,128)(2,1)S(1)} collective-permute-done((bf16[128,2048]{1,0:T(8,128)(2,1)}, bf16[128,2048]{1,0:T(8,128)(2,1)S(1)}, u32[]{:S(2)}, u32[]{:S(2)}) %collective-permute-start.4) | collective-permute-done | bytes 524320 | tf_op jit(solution)/shard_map/ppermute | solution.py:25
  101.2 3.6 %collective-permute-done.6.refs_6_.refs_7_ = bf16[128,2048]{1,0:T(8,128)(2,1)S(1)} collective-permute-done((bf16[128,2048]{1,0:T(8,128)(2,1)}, bf16[128,2048]{1,0:T(8,128)(2,1)S(1)}, u32[]{:S(2)}, u32[]{:S(2)}) %collective-permute-start.6) | collective-permute-done | bytes 524320 | tf_op jit(solution)/shard_map/ppermute | solution.py:25
  108.0 6.4 %dout.1 = (f32[1024,256]{1,0:T(8,128)}, bf16[1024,256]{1,0:T(8,128)(2,1)}) custom-call(bf16[128,2048]{1,0:T(8,128)(2,1)} %get-tuple-element.21.refs_4_.refs_2_.refs_0_, bf16[128,2048]{1,0:T(8,128)(2,1)} %copy-done.4, bf16[128,2048]{1,0:T(8,128)(2,1)} %copy-done.5, bf16[128,2048]{1,0:T(8,128)(2,1)} %collective-permute-done.2.refs_4_.refs_3_, ...), custom_call_target="tpu_custom_call" | custom-call | tf_op jit(solution)/shard_map/dout/pallas_call | solution.py:59
  114.5 6.2 %out_terms.1 = (bf16[4,2,512,128]{3,2,1,0:T(8,128)(2,1)}, bf16[4,2,512,128]{3,2,1,0:T(8,128)(2,1)}) custom-call(bf16[128,2048]{1,0:T(8,128)(2,1)} %get-tuple-element.21.refs_4_.refs_2_.refs_0_, bf16[128,2048]{1,0:T(8,128)(2,1)} %copy-done.4, bf16[128,2048]{1,0:T(8,128)(2,1)} %copy-done.5, bf16[128,2048]{1,0:T(8,128)(2,1)} %collective-permute-done.2.refs_4_.refs_3_, ...), custom_call_target="tpu_custom_call" | custom-call | tf_op jit(solution)/shard_map/out_terms/pallas_call | solution.py:59
  120.7 7.8 %collective-permute-done.10 = bf16[1024,256]{1,0:T(8,128)(2,1)S(1)} collective-permute-done((bf16[1024,256]{1,0:T(8,128)(2,1)}, bf16[1024,256]{1,0:T(8,128)(2,1)S(1)}, u32[]{:S(2)}, u32[]{:S(2)}) %collective-permute-start.10) | collective-permute-done | bytes 524320 | tf_op jit(solution)/shard_map/ppermute | solution.py:25
  129.4 8.1 %attention_backward.1.refs_1_.refs_0_ = bf16[768,1024]{1,0:T(8,128)(2,1)} custom-call(s32[8]{0:T(128)} %stack.152.refs_0_, bf16[8,144,768]{2,1,0:T(8,128)(2,1)} %copy-done, bf16[2,1024,1024]{2,1,0:T(8,128)(2,1)} %get-tuple-element.22.refs_2_, bf16[1024,256]{1,0:T(8,128)(2,1)} %add_convert_fusion.3.refs_3_, bf16[4,2,512,128]{3,2,1,0:T(8,128)(2,1)} %get-tuple-element.29.refs_4_), custom_call_target="tpu_custom_call" | custom-call | tf_op jit(solution)/shard_map/attention_backward/pallas_call | solution.py:59
  145.3 3.4 %collective-permute-start.12 = (bf16[2,512,128]{2,1,0:T(8,128)(2,1)S(1)}, bf16[2,512,128]{2,1,0:T(8,128)(2,1)S(1)}, u32[]{:S(2)}, u32[]{:S(2)}) collective-permute-start(bf16[2,512,128]{2,1,0:T(8,128)(2,1)S(1)} %get-tuple-element.41), channel_id=1, source_target_pairs={{32,0},{48,16},{0,32},{16,48},{33,1},{49,17},{1,33},{17,49},{34,2}... | collective-permute-start | bytes 786440 | tf_op jit(solution)/shard_map/ppermute | solution.py:25
  148.7 2.9 %collective-permute-done.14 = bf16[2,512,128]{2,1,0:T(8,128)(2,1)S(1)} collective-permute-done((bf16[2,512,128]{2,1,0:T(8,128)(2,1)S(1)}, bf16[2,512,128]{2,1,0:T(8,128)(2,1)S(1)}, u32[]{:S(2)}, u32[]{:S(2)}) %collective-permute-start.14) | collective-permute-done | bytes 262176 | tf_op jit(solution)/shard_map/ppermute | solution.py:25
  153.8 4.5 %collective-permute-done.12 = bf16[2,512,128]{2,1,0:T(8,128)(2,1)S(1)} collective-permute-done((bf16[2,512,128]{2,1,0:T(8,128)(2,1)S(1)}, bf16[2,512,128]{2,1,0:T(8,128)(2,1)S(1)}, u32[]{:S(2)}, u32[]{:S(2)}) %collective-permute-start.12) | collective-permute-done | bytes 262176 | tf_op jit(solution)/shard_map/ppermute | solution.py:25
  160.0 7.2 %term_blocks.2 = (bf16[4,2,768,128]{3,2,1,0:T(8,128)(2,1)}, bf16[4,2,768,128]{3,2,1,0:T(8,128)(2,1)}) custom-call(bf16[768,1024]{1,0:T(8,128)(2,1)} %attention_backward.1.refs_1_.refs_0_, bf16[1024,2048]{1,0:T(8,128)(2,1)} %all-gather.5.cloned.1.call-done.refs_1_, s32[5]{0:T(128)} %stack.158.refs_0_.refs_9_.refs_10_.refs_2_, bf16[2,512,128]{2,1,0:T(8,128)(2,1)} %fusion.1.refs_3_), custom_call_target="tpu_custom_call" | custom-call | tf_op jit(solution)/shard_map/term_blocks/pallas_call | solution.py:59
  167.3 7.4 %collective-permute-done.23.refs_0_ = bf16[768,1024]{1,0:T(8,128)(2,1)} collective-permute-done((bf16[768,1024]{1,0:T(8,128)(2,1)S(1)}, bf16[768,1024]{1,0:T(8,128)(2,1)}, u32[]{:S(2)}, u32[]{:S(2)}) %collective-permute-start.23) | collective-permute-done | bytes 1572896 | tf_op jit(solution)/shard_map/ppermute | solution.py:25
  174.6 7.4 %term_blocks.3 = (bf16[4,2,768,128]{3,2,1,0:T(8,128)(2,1)}, bf16[4,2,768,128]{3,2,1,0:T(8,128)(2,1)}) custom-call(bf16[768,1024]{1,0:T(8,128)(2,1)} %collective-permute-done.23.refs_0_, bf16[1024,2048]{1,0:T(8,128)(2,1)} %all-gather.5.cloned.1.call-done.refs_1_, s32[5]{0:T(128)} %stack.158.refs_0_.refs_9_.refs_10_.refs_2_, ...), custom_call_target="tpu_custom_call" | custom-call | tf_op jit(solution)/shard_map/term_blocks/pallas_call | solution.py:59
  184.7 3.4 %collective-permute-start.16 = (bf16[2,768,128]{2,1,0:T(8,128)(2,1)S(1)}, bf16[2,768,128]{2,1,0:T(8,128)(2,1)S(1)}, u32[]{:S(2)}, u32[]{:S(2)}) collective-permute-start(bf16[2,768,128]{2,1,0:T(8,128)(2,1)S(1)} %get-tuple-element.38), channel_id=1, source_target_pairs={{32,0},{48,16},{0,32},{16,48},{33,1},{49,17},{1,33},{17,49},{34,2}... | collective-permute-start | bytes 1179656 | tf_op jit(solution)/shard_map/ppermute | solution.py:25
  189.7 4.5 %collective-permute-done.18 = bf16[2,768,128]{2,1,0:T(8,128)(2,1)S(1)} collective-permute-done((bf16[2,768,128]{2,1,0:T(8,128)(2,1)S(1)}, bf16[2,768,128]{2,1,0:T(8,128)(2,1)S(1)}, u32[]{:S(2)}, u32[]{:S(2)}) %collective-permute-start.18) | collective-permute-done | bytes 393248 | tf_op jit(solution)/shard_map/ppermute | solution.py:25
  195.9 7.7 %collective-permute-done.16 = bf16[2,768,128]{2,1,0:T(8,128)(2,1)S(1)} collective-permute-done((bf16[2,768,128]{2,1,0:T(8,128)(2,1)S(1)}, bf16[2,768,128]{2,1,0:T(8,128)(2,1)S(1)}, u32[]{:S(2)}, u32[]{:S(2)}) %collective-permute-start.16) | collective-permute-done | bytes 393248 | tf_op jit(solution)/shard_map/ppermute | solution.py:25
  204.6 7.0 %all-to-all-start.1 = ((bf16[4,2,768,128]{3,2,1,0:T(8,128)(2,1)}), bf16[4,2,768,128]{3,2,1,0:T(8,128)(2,1)S(1)}, u32[]{:S(2)}, u32[]{:S(2)}) async-start(bf16[4,2,768,128]{3,2,1,0:T(8,128)(2,1)} %gate.6), calls=%async_computation.1 | async-start | bytes 3145728 | tf_op jit(solution)/shard_map/all_to_all | solution.py:371
  211.6 3.2 %collective-permute-start.28 = (bf16[256,128]{1,0:T(8,128)(2,1)S(1)}, bf16[256,128]{1,0:T(8,128)(2,1)S(1)}, u32[]{:S(2)}, u32[]{:S(2)}) collective-permute-start(bf16[256,128]{1,0:T(8,128)(2,1)S(1)} %get-tuple-element.53), channel_id=1, source_target_pairs={{0,68},{4,196},{64,4},{68,132},{128,64},{132,192},{192,0},{196,128... | collective-permute-start | bytes 196616 | tf_op jit(solution)/shard_map/ppermute | solution.py:35
  217.4 5.1 %collective-permute-start.25 = (bf16[256,128]{1,0:T(8,128)(2,1)S(1)}, bf16[256,128]{1,0:T(8,128)(2,1)S(1)}, u32[]{:S(2)}, u32[]{:S(2)}) collective-permute-start(bf16[256,128]{1,0:T(8,128)(2,1)S(1)} %get-tuple-element.50), channel_id=1, source_target_pairs={{0,0},{4,128},{64,64},{68,192},{128,4},{132,132},{192,68},{196,196... | collective-permute-start | bytes 196616 | tf_op jit(solution)/shard_map/ppermute | solution.py:35
  224.6 3.3 %collective-permute-start.21 = (bf16[768,128]{1,0:T(8,128)(2,1)S(1)}, bf16[768,128]{1,0:T(8,128)(2,1)S(1)}, u32[]{:S(2)}, u32[]{:S(2)}) collective-permute-start(bf16[768,128]{1,0:T(8,128)(2,1)S(1)} %get-tuple-element.46), channel_id=1, source_target_pairs={{0,0},{4,132},{64,64},{68,196},{1,1},{5,133},{65,65},{69,197},{2,2... | collective-permute-start | bytes 589832 | tf_op jit(solution)/shard_map/ppermute | solution.py:35
  239.9 13.9 %collective-permute-start.31 = (bf16[768,128]{1,0:T(8,128)(2,1)S(1)}, bf16[768,128]{1,0:T(8,128)(2,1)S(1)}, u32[]{:S(2)}, u32[]{:S(2)}) collective-permute-start(bf16[768,128]{1,0:T(8,128)(2,1)S(1)} %get-tuple-element.44), channel_id=1, source_target_pairs={{0,4},{4,128},{64,68},{68,192},{1,5},{5,129},{65,69},{69,193},{2,6... | collective-permute-start | bytes 589832 | tf_op jit(solution)/shard_map/ppermute | solution.py:35
  257.0 7.3 %collective-permute-done.32.refs_7_ = bf16[768,128]{1,0:T(8,128)(2,1)S(1)} collective-permute-done((bf16[768,128]{1,0:T(8,128)(2,1)S(1)}, bf16[768,128]{1,0:T(8,128)(2,1)S(1)}, u32[]{:S(2)}, u32[]{:S(2)}) %collective-permute-start.32) | collective-permute-done | bytes 196640 | tf_op jit(solution)/shard_map/ppermute | solution.py:35
  (129 shorter events, 60.4 us)
Async XLA Ops:
  7.2 97.6 %all-gather.3.cloned.1.call-start = ((), (), s32[]{:S(2)}) async-start(), calls=%async_computation.2 | async-start | bytes 2162688 | tf_op jit(solution)/shard_map/all_gather | solution.py:263
  7.2 9.4 %collective-permute-start.7 = (bf16[256,128]{1,0:T(8,128)(2,1)}, bf16[256,128]{1,0:T(8,128)(2,1)S(1)}, u32[]{:S(2)}, u32[]{:S(2)}) collective-permute-start(bf16[256,128]{1,0:T(8,128)(2,1)} %param.14), channel_id=1, source_target_pairs={{0,0},{4,128},{64,64},{68,192},{128,4},{132,132},{192,68},{196,196... | collective-permute-start | bytes 196616 | tf_op jit(solution)/shard_map/ppermute | solution.py:35
  25.4 49.3 %all-to-all-start = ((bf16[8,144,768]{2,1,0:T(8,128)(2,1)}), bf16[8,144,768]{2,1,0:T(8,128)(2,1)S(1)}, u32[]{:S(2)}, u32[]{:S(2)}) async-start(bf16[8,144,768]{2,1,0:T(8,128)(2,1)} %pack.1), calls=%async_computation | async-start | bytes 3538944 | tf_op jit(solution)/shard_map/all_to_all | solution.py:303
  31.3 128.7 %all-gather.5.cloned.1.call-start = ((), (), s32[]{:S(2)}) async-start(), calls=%async_computation.3 | async-start | bytes 5242880 | tf_op jit(solution)/shard_map/all_gather | solution.py:328
  31.3 30.9 %collective-permute-start = (bf16[128,2048]{1,0:T(8,128)(2,1)S(1)}, bf16[128,2048]{1,0:T(8,128)(2,1)S(1)}, u32[]{:S(2)}, u32[]{:S(2)}) collective-permute-start(bf16[128,2048]{1,0:T(8,128)(2,1)S(1)} %copy-done.2), channel_id=1, source_target_pairs={{1,0},{2,1},{3,2},{0,3},{5,4},{6,5},{7,6},{4,7},{9,8},{10,9},{11,1... | collective-permute-start | bytes 1572872 | tf_op jit(solution)/shard_map/ppermute | solution.py:25
  34.1 32.2 %collective-permute-start.1 = (bf16[128,2048]{1,0:T(8,128)(2,1)S(1)}, bf16[128,2048]{1,0:T(8,128)(2,1)S(1)}, u32[]{:S(2)}, u32[]{:S(2)}) collective-permute-start(bf16[128,2048]{1,0:T(8,128)(2,1)S(1)} %copy-done.2), channel_id=1, source_target_pairs={{2,0},{3,1},{0,2},{1,3},{6,4},{7,5},{4,6},{5,7},{10,8},{11,9},{8,1... | collective-permute-start | bytes 1572872 | tf_op jit(solution)/shard_map/ppermute | solution.py:25
  34.9 39.8 %collective-permute-start.2 = (bf16[128,2048]{1,0:T(8,128)(2,1)S(1)}, bf16[128,2048]{1,0:T(8,128)(2,1)}, u32[]{:S(2)}, u32[]{:S(2)}) collective-permute-start(bf16[128,2048]{1,0:T(8,128)(2,1)S(1)} %copy-done.2), channel_id=1, source_target_pairs={{3,0},{0,1},{1,2},{2,3},{7,4},{4,5},{5,6},{6,7},{11,8},{8,9},{9,10... | collective-permute-start | bytes 1572872 | tf_op jit(solution)/shard_map/ppermute | solution.py:25
  35.8 38.9 %collective-permute-start.3 = (bf16[128,2048]{1,0:T(8,128)(2,1)}, bf16[128,2048]{1,0:T(8,128)(2,1)}, u32[]{:S(2)}, u32[]{:S(2)}) collective-permute-start(bf16[128,2048]{1,0:T(8,128)(2,1)} %get-tuple-element.23), channel_id=1, source_target_pairs={{4,0},{0,4},{5,1},{1,5},{6,2},{2,6},{7,3},{3,7},{12,8},{8,12},{13,... | collective-permute-start | bytes 1572872 | tf_op jit(solution)/shard_map/ppermute | solution.py:25
  39.5 52.3 %collective-permute-start.8 = (bf16[128,2048]{1,0:T(8,128)(2,1)}, bf16[128,2048]{1,0:T(8,128)(2,1)}, u32[]{:S(2)}, u32[]{:S(2)}) collective-permute-start(bf16[128,2048]{1,0:T(8,128)(2,1)} %get-tuple-element.25), channel_id=1, source_target_pairs={{4,0},{0,4},{5,1},{1,5},{6,2},{2,6},{7,3},{3,7},{12,8},{8,12},{13,... | collective-permute-start | bytes 1572872 | tf_op jit(solution)/shard_map/ppermute | solution.py:25
  76.0 25.2 %collective-permute-start.4 = (bf16[128,2048]{1,0:T(8,128)(2,1)}, bf16[128,2048]{1,0:T(8,128)(2,1)S(1)}, u32[]{:S(2)}, u32[]{:S(2)}) collective-permute-start(bf16[128,2048]{1,0:T(8,128)(2,1)} %gate.4.refs_4_), channel_id=1, source_target_pairs={{1,0},{2,1},{3,2},{0,3},{5,4},{6,5},{7,6},{4,7},{9,8},{10,9},{11,1... | collective-permute-start | bytes 1572872 | tf_op jit(solution)/shard_map/ppermute | solution.py:25
  78.1 23.1 %collective-permute-start.5 = (bf16[128,2048]{1,0:T(8,128)(2,1)}, bf16[128,2048]{1,0:T(8,128)(2,1)S(1)}, u32[]{:S(2)}, u32[]{:S(2)}) collective-permute-start(bf16[128,2048]{1,0:T(8,128)(2,1)} %gate.4.refs_4_), channel_id=1, source_target_pairs={{2,0},{3,1},{0,2},{1,3},{6,4},{7,5},{4,6},{5,7},{10,8},{11,9},{8,1... | collective-permute-start | bytes 1572872 | tf_op jit(solution)/shard_map/ppermute | solution.py:25
  79.6 25.2 %collective-permute-start.6 = (bf16[128,2048]{1,0:T(8,128)(2,1)}, bf16[128,2048]{1,0:T(8,128)(2,1)S(1)}, u32[]{:S(2)}, u32[]{:S(2)}) collective-permute-start(bf16[128,2048]{1,0:T(8,128)(2,1)} %gate.4.refs_4_), channel_id=1, source_target_pairs={{3,0},{0,1},{1,2},{2,3},{7,4},{4,5},{5,6},{6,7},{11,8},{8,9},{9,10... | collective-permute-start | bytes 1572872 | tf_op jit(solution)/shard_map/ppermute | solution.py:25
  89.8 14.9 %collective-permute-start.9 = (bf16[256,1024]{1,0:T(8,128)(2,1)}, bf16[256,1024]{1,0:T(8,128)(2,1)S(1)}, u32[]{:S(2)}, u32[]{:S(2)}) collective-permute-start(bf16[256,1024]{1,0:T(8,128)(2,1)} %get-tuple-element.26.refs_8_), channel_id=1, source_target_pairs={{4,0},{0,4},{5,1},{1,5},{6,2},{2,6},{7,3},{3,7},{12,8},{8,12},{13,... | collective-permute-start | bytes 1572872 | tf_op jit(solution)/shard_map/ppermute | solution.py:25
  114.5 14.1 %collective-permute-start.10 = (bf16[1024,256]{1,0:T(8,128)(2,1)}, bf16[1024,256]{1,0:T(8,128)(2,1)S(1)}, u32[]{:S(2)}, u32[]{:S(2)}) collective-permute-start(bf16[1024,256]{1,0:T(8,128)(2,1)} %get-tuple-element.28.refs_11_), channel_id=1, source_target_pairs={{4,0},{0,4},{5,1},{1,5},{6,2},{2,6},{7,3},{3,7},{12,8},{8,12},{13,... | collective-permute-start | bytes 1572872 | tf_op jit(solution)/shard_map/ppermute | solution.py:25
  138.9 35.7 %collective-permute-start.23 = (bf16[768,1024]{1,0:T(8,128)(2,1)S(1)}, bf16[768,1024]{1,0:T(8,128)(2,1)}, u32[]{:S(2)}, u32[]{:S(2)}) collective-permute-start(bf16[768,1024]{1,0:T(8,128)(2,1)S(1)} %copy-done.1), channel_id=1, source_target_pairs={{4,0},{0,4},{5,1},{1,5},{6,2},{2,6},{7,3},{3,7},{12,8},{8,12},{13,... | collective-permute-start | bytes 4718600 | tf_op jit(solution)/shard_map/ppermute | solution.py:25
  143.7 10.1 %collective-permute-start.13 = (bf16[2,512,128]{2,1,0:T(8,128)(2,1)S(1)}, bf16[2,512,128]{2,1,0:T(8,128)(2,1)S(1)}, u32[]{:S(2)}, u32[]{:S(2)}) collective-permute-start(bf16[2,512,128]{2,1,0:T(8,128)(2,1)S(1)} %get-tuple-element.43), channel_id=1, source_target_pairs={{48,0},{0,16},{16,32},{32,48},{49,1},{1,17},{17,33},{33,49},{50,2}... | collective-permute-start | bytes 786440 | tf_op jit(solution)/shard_map/ppermute | solution.py:25
  145.3 13.0 %collective-permute-start.12 = (bf16[2,512,128]{2,1,0:T(8,128)(2,1)S(1)}, bf16[2,512,128]{2,1,0:T(8,128)(2,1)S(1)}, u32[]{:S(2)}, u32[]{:S(2)}) collective-permute-start(bf16[2,512,128]{2,1,0:T(8,128)(2,1)S(1)} %get-tuple-element.41), channel_id=1, source_target_pairs={{32,0},{48,16},{0,32},{16,48},{33,1},{49,17},{1,33},{17,49},{34,2}... | collective-permute-start | bytes 786440 | tf_op jit(solution)/shard_map/ppermute | solution.py:25
  167.3 14.8 %collective-permute-start.15 = (bf16[4,2,768,128]{3,2,1,0:T(8,128)(2,1)}, bf16[4,2,768,128]{3,2,1,0:T(8,128)(2,1)S(1)}, u32[]{:S(2)}, u32[]{:S(2)}) collective-permute-start(bf16[4,2,768,128]{3,2,1,0:T(8,128)(2,1)} %get-tuple-element.32), channel_id=1, source_target_pairs={{8,0},{0,8},{9,1},{1,9},{10,2},{2,10},{11,3},{3,11},{12,4},{4,12},... | collective-permute-start | bytes 4718600 | tf_op jit(solution)/shard_map/ppermute | solution.py:25
  182.6 11.6 %collective-permute-start.18 = (bf16[2,768,128]{2,1,0:T(8,128)(2,1)S(1)}, bf16[2,768,128]{2,1,0:T(8,128)(2,1)S(1)}, u32[]{:S(2)}, u32[]{:S(2)}) collective-permute-start(bf16[2,768,128]{2,1,0:T(8,128)(2,1)S(1)} %get-tuple-element.39), channel_id=1, source_target_pairs={{16,0},{32,16},{48,32},{0,48},{17,1},{33,17},{49,33},{1,49},{18,2}... | collective-permute-start | bytes 1179656 | tf_op jit(solution)/shard_map/ppermute | solution.py:25
  183.1 12.8 %collective-permute-start.17 = (bf16[2,768,128]{2,1,0:T(8,128)(2,1)S(1)}, bf16[2,768,128]{2,1,0:T(8,128)(2,1)S(1)}, u32[]{:S(2)}, u32[]{:S(2)}) collective-permute-start(bf16[2,768,128]{2,1,0:T(8,128)(2,1)S(1)} %get-tuple-element.40), channel_id=1, source_target_pairs={{48,0},{0,16},{16,32},{32,48},{49,1},{1,17},{17,33},{33,49},{50,2}... | collective-permute-start | bytes 1179656 | tf_op jit(solution)/shard_map/ppermute | solution.py:25
  184.7 18.9 %collective-permute-start.16 = (bf16[2,768,128]{2,1,0:T(8,128)(2,1)S(1)}, bf16[2,768,128]{2,1,0:T(8,128)(2,1)S(1)}, u32[]{:S(2)}, u32[]{:S(2)}) collective-permute-start(bf16[2,768,128]{2,1,0:T(8,128)(2,1)S(1)} %get-tuple-element.38), channel_id=1, source_target_pairs={{32,0},{48,16},{0,32},{16,48},{33,1},{49,17},{1,33},{17,49},{34,2}... | collective-permute-start | bytes 1179656 | tf_op jit(solution)/shard_map/ppermute | solution.py:25
  204.6 26.6 %all-to-all-start.1 = ((bf16[4,2,768,128]{3,2,1,0:T(8,128)(2,1)}), bf16[4,2,768,128]{3,2,1,0:T(8,128)(2,1)S(1)}, u32[]{:S(2)}, u32[]{:S(2)}) async-start(bf16[4,2,768,128]{3,2,1,0:T(8,128)(2,1)} %gate.6), calls=%async_computation.1 | async-start | bytes 3145728 | tf_op jit(solution)/shard_map/all_to_all | solution.py:371
  211.6 12.3 %collective-permute-start.28 = (bf16[256,128]{1,0:T(8,128)(2,1)S(1)}, bf16[256,128]{1,0:T(8,128)(2,1)S(1)}, u32[]{:S(2)}, u32[]{:S(2)}) collective-permute-start(bf16[256,128]{1,0:T(8,128)(2,1)S(1)} %get-tuple-element.53), channel_id=1, source_target_pairs={{0,68},{4,196},{64,4},{68,132},{128,64},{132,192},{192,0},{196,128... | collective-permute-start | bytes 196616 | tf_op jit(solution)/shard_map/ppermute | solution.py:35
  214.8 9.7 %collective-permute-start.27 = (bf16[256,128]{1,0:T(8,128)(2,1)S(1)}, bf16[256,128]{1,0:T(8,128)(2,1)S(1)}, u32[]{:S(2)}, u32[]{:S(2)}) collective-permute-start(bf16[256,128]{1,0:T(8,128)(2,1)S(1)} %get-tuple-element.52), channel_id=1, source_target_pairs={{0,64},{4,192},{64,0},{68,128},{128,68},{132,196},{192,4},{196,132... | collective-permute-start | bytes 196616 | tf_op jit(solution)/shard_map/ppermute | solution.py:35
  214.9 12.9 %collective-permute-start.26 = (bf16[256,128]{1,0:T(8,128)(2,1)S(1)}, bf16[256,128]{1,0:T(8,128)(2,1)S(1)}, u32[]{:S(2)}, u32[]{:S(2)}) collective-permute-start(bf16[256,128]{1,0:T(8,128)(2,1)S(1)} %get-tuple-element.51), channel_id=1, source_target_pairs={{0,4},{4,132},{64,68},{68,196},{128,0},{132,128},{192,64},{196,192... | collective-permute-start | bytes 196616 | tf_op jit(solution)/shard_map/ppermute | solution.py:35
  217.4 13.1 %collective-permute-start.25 = (bf16[256,128]{1,0:T(8,128)(2,1)S(1)}, bf16[256,128]{1,0:T(8,128)(2,1)S(1)}, u32[]{:S(2)}, u32[]{:S(2)}) collective-permute-start(bf16[256,128]{1,0:T(8,128)(2,1)S(1)} %get-tuple-element.50), channel_id=1, source_target_pairs={{0,0},{4,128},{64,64},{68,192},{128,4},{132,132},{192,68},{196,196... | collective-permute-start | bytes 196616 | tf_op jit(solution)/shard_map/ppermute | solution.py:35
  222.6 9.7 %collective-permute-start.19 = (bf16[768,128]{1,0:T(8,128)(2,1)S(1)}, bf16[768,128]{1,0:T(8,128)(2,1)S(1)}, u32[]{:S(2)}, u32[]{:S(2)}) collective-permute-start(bf16[768,128]{1,0:T(8,128)(2,1)S(1)} %get-tuple-element.47), channel_id=1, source_target_pairs={{0,64},{4,196},{64,0},{68,132},{1,65},{5,197},{65,1},{69,133},{2,6... | collective-permute-start | bytes 589832 | tf_op jit(solution)/shard_map/ppermute | solution.py:35
  224.6 9.4 %collective-permute-start.21 = (bf16[768,128]{1,0:T(8,128)(2,1)S(1)}, bf16[768,128]{1,0:T(8,128)(2,1)S(1)}, u32[]{:S(2)}, u32[]{:S(2)}) collective-permute-start(bf16[768,128]{1,0:T(8,128)(2,1)S(1)} %get-tuple-element.46), channel_id=1, source_target_pairs={{0,0},{4,132},{64,64},{68,196},{1,1},{5,133},{65,65},{69,197},{2,2... | collective-permute-start | bytes 589832 | tf_op jit(solution)/shard_map/ppermute | solution.py:35
  236.4 18.7 %collective-permute-start.29 = (bf16[768,128]{1,0:T(8,128)(2,1)S(1)}, bf16[768,128]{1,0:T(8,128)(2,1)S(1)}, u32[]{:S(2)}, u32[]{:S(2)}) collective-permute-start(bf16[768,128]{1,0:T(8,128)(2,1)S(1)} %get-tuple-element.45), channel_id=1, source_target_pairs={{0,68},{4,192},{64,4},{68,128},{1,69},{5,193},{65,5},{69,129},{2,7... | collective-permute-start | bytes 589832 | tf_op jit(solution)/shard_map/ppermute | solution.py:35
  238.6 16.5 %collective-permute-start.30 = (bf16[768,128]{1,0:T(8,128)(2,1)S(1)}, bf16[768,128]{1,0:T(8,128)(2,1)S(1)}, u32[]{:S(2)}, u32[]{:S(2)}) collective-permute-start(bf16[768,128]{1,0:T(8,128)(2,1)S(1)} %get-tuple-element.45), channel_id=1, source_target_pairs={{128,68},{132,192},{192,4},{196,128},{129,69},{133,193},{193,5},{1... | collective-permute-start | bytes 589832 | tf_op jit(solution)/shard_map/ppermute | solution.py:35
  239.9 17.1 %collective-permute-start.31 = (bf16[768,128]{1,0:T(8,128)(2,1)S(1)}, bf16[768,128]{1,0:T(8,128)(2,1)S(1)}, u32[]{:S(2)}, u32[]{:S(2)}) collective-permute-start(bf16[768,128]{1,0:T(8,128)(2,1)S(1)} %get-tuple-element.44), channel_id=1, source_target_pairs={{0,4},{4,128},{64,68},{68,192},{1,5},{5,129},{65,69},{69,193},{2,6... | collective-permute-start | bytes 589832 | tf_op jit(solution)/shard_map/ppermute | solution.py:35
  253.8 10.6 %collective-permute-start.32 = (bf16[768,128]{1,0:T(8,128)(2,1)S(1)}, bf16[768,128]{1,0:T(8,128)(2,1)S(1)}, u32[]{:S(2)}, u32[]{:S(2)}) collective-permute-start(bf16[768,128]{1,0:T(8,128)(2,1)S(1)} %get-tuple-element.44), channel_id=1, source_target_pairs={{128,4},{132,128},{192,68},{196,192},{129,5},{133,129},{193,69},{1... | collective-permute-start | bytes 589832 | tf_op jit(solution)/shard_map/ppermute | solution.py:35
  (30 other events, 158.6 us)
Sparse Core Ops, SparseCore 0:
  17.4 59.4 all-gather.2
  108.2 50.0 all-gather.4

commit v2 on v1

--- a/solution.py
+++ b/solution.py
@@ -231,11 +231,13 @@
 
 
 def finish_kernel(*refs):
+    parts, outs = refs[:8], refs[8:]
     for head in range(2):
         for j in range(3):
             rows = slice((head * 3 + j) * HEAD, (head * 3 + j + 1) * HEAD)
-            total = sum(r[rows, :].astype(F32) for r in refs[:8])
-            refs[8 + j][:, head * HEAD : (head + 1) * HEAD] = total.T
+            total = sum(r[rows, :].astype(F32) for r in parts)
+            outs[j][:, head * HEAD : (head + 1) * HEAD] = total.T
+    outs[3][...] = sum(r[768:, :].astype(F32) for r in parts)
 
 
 def add_low(a, b):
@@ -367,47 +369,39 @@
     def core_sum(send, keep):
         return add_low(keep, recv(send, "c", 1))
 
-    def y_sum(blocks):
-        arrived = lax.all_to_all(blocks, "y", split_axis=0, concat_axis=0, tiled=True)
-        return jnp.sum(arrived.astype(F32), axis=0).astype(BF16)
-
     def y_permuted(blocks):
         part = 0.0
         for dy in (2, 1, 3, 0):
             block = lax.dynamic_index_in_dim(blocks, (y + dy) % 4, 0, keepdims=False)
             part = part + (recv(block, "y", 4 - dy) if dy else block).astype(F32)
-        return part.astype(BF16)
-
-    out_part = y_permuted(core_sum(gate(out_send, [terms_t]), out_keep))
+        return part
+
+    out_part = y_permuted(core_sum(gate(out_send, [terms_t]), out_keep)).astype(BF16)
 
     send, keep = term_blocks(terms_t, slab, place, False, [out_part])
     part = y_permuted(core_sum(send, keep))
-    full = []
+    full, own_sums = [], []
     for i, a in enumerate((1, 0)):
+        both = jnp.concatenate([part[i].astype(BF16), out_part[a, :256]], axis=0)
+        own_sums.append(both)
         for s in range(2):
-            full.append(send_zz(part[i], lambda h1, h0, l: (l, h0 ^ a, l), s))
-
-    grad_out = 0.0
-    for a in range(2):
-        for b in range(2):
-            chosen = lax.dynamic_slice_in_dim(out_part[a], (h // 2 + b + l) % 2 * 256, 256, 0)
-            chosen = send_zz(chosen, lambda h1, h0, l: (l, h0 ^ a, h1 ^ b))
-            grad_out = grad_out + chosen.astype(F32)
-
-    blocks = gate(core_sum(*term_blocks(terms_pair, slab, place, True, [keep])), [part])
-    part = gate(y_sum(blocks), [grad_out] + full)
+            full.append(send_zz(both, lambda h1, h0, l: (l, h0 ^ a, l), s))
+    own = full[:]
+    blocks = gate(core_sum(*term_blocks(terms_pair, slab, place, True, [keep])), own_sums)
+    arrived = lax.all_to_all(blocks, "y", split_axis=0, concat_axis=0, tiled=True)
     for i, a in enumerate((1, 0)):
+        total = jnp.sum(arrived[:, i].astype(F32), axis=0).astype(BF16)
+        both = gate(jnp.concatenate([total, out_part[a, 256:]], axis=0), own[2 * i : 2 * i + 2])
         for s in range(2):
-            full.append(send_zz(part[i], lambda h1, h0, l: (l, h0 ^ a, 1 - l), s))
-    grad_q, grad_k, grad_v = call(
+            full.append(send_zz(both, lambda h1, h0, l: (l, h0 ^ a, 1 - l), s))
+    return call(
         finish_kernel,
         "finish",
         full,
         [VMEM] * 8,
-        tuple(shape(128, 256, dtype=F32) for _ in range(3)),
-        (VMEM,) * 3,
-    )
-    return grad_q, grad_k, grad_v, grad_out
+        tuple(shape(128, 256, dtype=F32) for _ in range(3)) + (shape(256, 128, dtype=F32),),
+        (VMEM,) * 4,
+    )
 
 
 def solution(mesh):

time: 275 us -> 273 us (level)
  starting transfers between devices: 77.9 us -> 58.5 us
  waiting for transfers between devices: 102 us -> 115 us
    all_to_all x1, waiting for transfers between devices: 0.01 us -> 19.7 us  [shards(): lax.all_to_all(to_heads, SEQ, split_axis=0, concat_axis=0, tiled=True)]
    ppermute x20, waiting for transfers between devices: 85.9 us -> 69.3 us  [recv(): return lax.ppermute(block, axis, [((i + offset) % n, i) for i in range(n)])]
    ppermute x13 -> x9, starting transfers between devices: 41.5 us -> 28.1 us  [send_zz(): return lax.ppermute(block, ('h', 'l'), pairs)]
    all_to_all x1, waiting for transfers between devices: 0.01 us -> 11.6 us  [shards(): lax.all_to_all(blocks, 'y', split_axis=0, concat_axis=0, tiled=True)]
    ppermute x20, starting transfers between devices: 23.6 us -> 19.8 us  [recv(): return lax.ppermute(block, axis, [((i + offset) % n, i) for i in range(n)])]
    concatenate x0 -> x4, other arithmetic: none -> 2.89 us  [the longest x2 1.46 us: shards(): both = jnp.concatenate([part[i].astype(BF16), out_part[a, :256]], axis=0)]
    ppermute x13 -> x9, waiting for transfers between devices: 16.3 us -> 14.3 us  [send_zz(): return lax.ppermute(block, ('h', 'l'), pairs)]
    unnamed x50 -> x52, local copies, waits for them, and re-layouts: 7.21 us -> 8.47 us
  transfers between devices with their start and end apart: 37 -> 33, of which waited for: 19 -> 17; matrix products, arithmetic and copies ran while one was open for 4% -> 5% of each run, Pallas kernels for 19% -> 20%
where the time goes in v2:
time: 273 us; the launch traced here: 270 us
  waiting for transfers between devices  115 us (42%)
  starting transfers between devices  58.5 us (21%)
  Pallas kernels  58.2 us (21%)
  between operations  15.1 us (6%)
  other arithmetic  11.6 us (4%)
  local copies, waits for them, and re-layouts  11.4 us (4%)
    ppermute x20, waiting for transfers between devices, recv(): return lax.ppermute(block, axis, [((i + offset) % n, i) for i in range(n)])  69.3 us
    pallas_call x11, Pallas kernels, call(): pl.pallas_call(body, grid=grid, out_shape=outs, in_specs=[whole(s, a) for...  58.2 us
    ppermute x9, starting transfers between devices, send_zz(): return lax.ppermute(block, ('h', 'l'), pairs)  28.1 us
    ppermute x20, starting transfers between devices, recv(): return lax.ppermute(block, axis, [((i + offset) % n, i) for i in range(n)])  19.8 us
    all_to_all x1, waiting for transfers between devices, shards(): lax.all_to_all(to_heads, SEQ, split_axis=0, concat_axis=0, tiled=True)  19.7 us
    ppermute x9, waiting for transfers between devices, send_zz(): return lax.ppermute(block, ('h', 'l'), pairs)  14.3 us
    all_to_all x1, waiting for transfers between devices, shards(): lax.all_to_all(blocks, 'y', split_axis=0, concat_axis=0, tiled=True)  11.6 us
    unnamed x52, local copies, waits for them, and re-layouts  8.47 us
  transfers between devices with their start and end apart: 33, of which 17 were waited for; matrix products, arithmetic and copies ran while one was open for 5% of the time, Pallas kernels for 20%

profile of v2, /device:TPU:104, one launch (start us, length us, event | category | flops | bytes accessed | tf_op | source)
XLA Modules:
  0.0 269.7 jit_solution(973125677197368918)
XLA Ops:
  7.2 5.9 %collective-permute-start.7 = (bf16[256,128]{1,0:T(8,128)(2,1)}, bf16[256,128]{1,0:T(8,128)(2,1)S(1)}, u32[]{:S(2)}, u32[]{:S(2)}) collective-permute-start(bf16[256,128]{1,0:T(8,128)(2,1)} %param.14), channel_id=1, source_target_pairs={{0,0},{4,128},{64,64},{68,192},{128,4},{132,132},{192,68},{196,196... | collective-permute-start | bytes 196616 | tf_op jit(solution)/shard_map/ppermute | solution.py:35
  13.2 3.4 %collective-permute-done.7 = bf16[256,128]{1,0:T(8,128)(2,1)S(1)} collective-permute-done((bf16[256,128]{1,0:T(8,128)(2,1)}, bf16[256,128]{1,0:T(8,128)(2,1)S(1)}, u32[]{:S(2)}, u32[]{:S(2)}) %collective-permute-start.7) | collective-permute-done | bytes 65568 | tf_op jit(solution)/shard_map/ppermute | solution.py:35
  20.0 2.4 scale.1
  22.5 2.9 %pack.1 = bf16[8,144,768]{2,1,0:T(8,128)(2,1)} custom-call(bf16[128,2048]{1,0:T(8,128)(2,1)} %refs_0_.1, bf16[128,2048]{1,0:T(8,128)(2,1)} %refs_1_.4, bf16[128,2048]{1,0:T(8,128)(2,1)} %refs_2_.1, s32[1,128]{1,0:T(1,128)} %refs_3_.1, bf16[128,2048]{1,0:T(8,128)(2,1)} %get-tuple-element.18.refs_4_.refs_2_.refs_0_), custom_call_target="tpu_custom_call" | custom-call | tf_op jit(solution)/shard_map/pack/pallas_call | solution.py:59
  25.4 5.9 %all-to-all-start = ((bf16[8,144,768]{2,1,0:T(8,128)(2,1)}), bf16[8,144,768]{2,1,0:T(8,128)(2,1)S(1)}, u32[]{:S(2)}, u32[]{:S(2)}) async-start(bf16[8,144,768]{2,1,0:T(8,128)(2,1)} %pack.1), calls=%async_computation | async-start | bytes 3538944 | tf_op jit(solution)/shard_map/all_to_all | solution.py:305
  31.3 2.8 %collective-permute-start = (bf16[128,2048]{1,0:T(8,128)(2,1)S(1)}, bf16[128,2048]{1,0:T(8,128)(2,1)S(1)}, u32[]{:S(2)}, u32[]{:S(2)}) collective-permute-start(bf16[128,2048]{1,0:T(8,128)(2,1)S(1)} %copy-done.2), channel_id=1, source_target_pairs={{1,0},{2,1},{3,2},{0,3},{5,4},{6,5},{7,6},{4,7},{9,8},{10,9},{11,1... | collective-permute-start | bytes 1572872 | tf_op jit(solution)/shard_map/ppermute | solution.py:25
  37.0 2.5 reorder.1
  41.6 19.7 %all-to-all-done.refs_1_ = bf16[8,144,768]{2,1,0:T(8,128)(2,1)S(1)} async-done(((bf16[8,144,768]{2,1,0:T(8,128)(2,1)}), bf16[8,144,768]{2,1,0:T(8,128)(2,1)S(1)}, u32[]{:S(2)}, u32[]{:S(2)}) %all-to-all-start) | async-done | bytes 1769504 | tf_op jit(solution)/shard_map/all_to_all | solution.py:305
  62.6 10.2 %attention_forward.1 = (bf16[256,1024]{1,0:T(8,128)(2,1)}, bf16[2,1024,1024]{2,1,0:T(8,128)(2,1)}) custom-call(s32[8]{0:T(128)} %stack.152.refs_0_, bf16[8,144,768]{2,1,0:T(8,128)(2,1)} %copy-done), custom_call_target="tpu_custom_call" | custom-call | tf_op jit(solution)/shard_map/attention_forward/pallas_call | solution.py:59
  78.3 6.9 %collective-permute-done.8.refs_1_ = bf16[128,2048]{1,0:T(8,128)(2,1)} collective-permute-done((bf16[128,2048]{1,0:T(8,128)(2,1)}, bf16[128,2048]{1,0:T(8,128)(2,1)}, u32[]{:S(2)}, u32[]{:S(2)}) %collective-permute-start.8) | collective-permute-done | bytes 524320 | tf_op jit(solution)/shard_map/ppermute | solution.py:25
  85.1 8.8 %collective-permute-done.9.refs_2_.refs_9_ = bf16[256,1024]{1,0:T(8,128)(2,1)S(1)} collective-permute-done((bf16[256,1024]{1,0:T(8,128)(2,1)}, bf16[256,1024]{1,0:T(8,128)(2,1)S(1)}, u32[]{:S(2)}, u32[]{:S(2)}) %collective-permute-start.9) | collective-permute-done | bytes 524320 | tf_op jit(solution)/shard_map/ppermute | solution.py:25
  94.0 5.9 %collective-permute-done.4.refs_4_.refs_5_ = bf16[128,2048]{1,0:T(8,128)(2,1)S(1)} collective-permute-done((bf16[128,2048]{1,0:T(8,128)(2,1)}, bf16[128,2048]{1,0:T(8,128)(2,1)S(1)}, u32[]{:S(2)}, u32[]{:S(2)}) %collective-permute-start.4) | collective-permute-done | bytes 524320 | tf_op jit(solution)/shard_map/ppermute | solution.py:25
  99.8 3.6 %collective-permute-done.6.refs_6_.refs_7_ = bf16[128,2048]{1,0:T(8,128)(2,1)S(1)} collective-permute-done((bf16[128,2048]{1,0:T(8,128)(2,1)}, bf16[128,2048]{1,0:T(8,128)(2,1)S(1)}, u32[]{:S(2)}, u32[]{:S(2)}) %collective-permute-start.6) | collective-permute-done | bytes 524320 | tf_op jit(solution)/shard_map/ppermute | solution.py:25
  106.5 6.4 %dout.1 = (f32[1024,256]{1,0:T(8,128)}, bf16[1024,256]{1,0:T(8,128)(2,1)}) custom-call(bf16[128,2048]{1,0:T(8,128)(2,1)} %get-tuple-element.18.refs_4_.refs_2_.refs_0_, bf16[128,2048]{1,0:T(8,128)(2,1)} %copy-done.4, bf16[128,2048]{1,0:T(8,128)(2,1)} %copy-done.5, bf16[128,2048]{1,0:T(8,128)(2,1)} %collective-permute-done.2.refs_4_.refs_3_, ...), custom_call_target="tpu_custom_call" | custom-call | tf_op jit(solution)/shard_map/dout/pallas_call | solution.py:59
  112.9 6.2 %out_terms.1 = (bf16[4,2,512,128]{3,2,1,0:T(8,128)(2,1)}, bf16[4,2,512,128]{3,2,1,0:T(8,128)(2,1)}) custom-call(bf16[128,2048]{1,0:T(8,128)(2,1)} %get-tuple-element.18.refs_4_.refs_2_.refs_0_, bf16[128,2048]{1,0:T(8,128)(2,1)} %copy-done.4, bf16[128,2048]{1,0:T(8,128)(2,1)} %copy-done.5, bf16[128,2048]{1,0:T(8,128)(2,1)} %collective-permute-done.2.refs_4_.refs_3_, ...), custom_call_target="tpu_custom_call" | custom-call | tf_op jit(solution)/shard_map/out_terms/pallas_call | solution.py:59
  119.1 7.8 %collective-permute-done.10 = bf16[1024,256]{1,0:T(8,128)(2,1)S(1)} collective-permute-done((bf16[1024,256]{1,0:T(8,128)(2,1)}, bf16[1024,256]{1,0:T(8,128)(2,1)S(1)}, u32[]{:S(2)}, u32[]{:S(2)}) %collective-permute-start.10) | collective-permute-done | bytes 524320 | tf_op jit(solution)/shard_map/ppermute | solution.py:25
  127.9 8.1 %attention_backward.1.refs_1_.refs_0_ = bf16[768,1024]{1,0:T(8,128)(2,1)} custom-call(s32[8]{0:T(128)} %stack.152.refs_0_, bf16[8,144,768]{2,1,0:T(8,128)(2,1)} %copy-done, bf16[2,1024,1024]{2,1,0:T(8,128)(2,1)} %get-tuple-element.19.refs_2_, bf16[1024,256]{1,0:T(8,128)(2,1)} %add_convert_fusion.3.refs_3_, bf16[4,2,512,128]{3,2,1,0:T(8,128)(2,1)} %get-tuple-element.26.refs_4_), custom_call_target="tpu_custom_call" | custom-call | tf_op jit(solution)/shard_map/attention_backward/pallas_call | solution.py:59
  146.0 6.4 %collective-permute-done.12 = bf16[2,512,128]{2,1,0:T(8,128)(2,1)S(1)} collective-permute-done((bf16[2,512,128]{2,1,0:T(8,128)(2,1)S(1)}, bf16[2,512,128]{2,1,0:T(8,128)(2,1)S(1)}, u32[]{:S(2)}, u32[]{:S(2)}) %collective-permute-start.12) | collective-permute-done | bytes 262176 | tf_op jit(solution)/shard_map/ppermute | solution.py:25
  152.4 4.9 %collective-permute-done.13 = bf16[2,512,128]{2,1,0:T(8,128)(2,1)S(1)} collective-permute-done((bf16[2,512,128]{2,1,0:T(8,128)(2,1)S(1)}, bf16[2,512,128]{2,1,0:T(8,128)(2,1)S(1)}, u32[]{:S(2)}, u32[]{:S(2)}) %collective-permute-start.13) | collective-permute-done | bytes 262176 | tf_op jit(solution)/shard_map/ppermute | solution.py:25
  159.2 7.3 %term_blocks.2 = (bf16[4,2,768,128]{3,2,1,0:T(8,128)(2,1)}, bf16[4,2,768,128]{3,2,1,0:T(8,128)(2,1)}) custom-call(bf16[768,1024]{1,0:T(8,128)(2,1)} %attention_backward.1.refs_1_.refs_0_, bf16[1024,2048]{1,0:T(8,128)(2,1)} %all-gather.5.cloned.1.call-done.refs_1_, s32[5]{0:T(128)} %stack.158.refs_0_.refs_9_.refs_10_.refs_2_, bf16[2,512,128]{2,1,0:T(8,128)(2,1)} %fusion.1.refs_3_), custom_call_target="tpu_custom_call" | custom-call | tf_op jit(solution)/shard_map/term_blocks/pallas_call | solution.py:59
  166.4 6.6 %collective-permute-done.23.refs_0_ = bf16[768,1024]{1,0:T(8,128)(2,1)} collective-permute-done((bf16[768,1024]{1,0:T(8,128)(2,1)S(1)}, bf16[768,1024]{1,0:T(8,128)(2,1)}, u32[]{:S(2)}, u32[]{:S(2)}) %collective-permute-start.23) | collective-permute-done | bytes 1572896 | tf_op jit(solution)/shard_map/ppermute | solution.py:25
  173.1 7.4 %term_blocks.3 = (bf16[4,2,768,128]{3,2,1,0:T(8,128)(2,1)}, bf16[4,2,768,128]{3,2,1,0:T(8,128)(2,1)}) custom-call(bf16[768,1024]{1,0:T(8,128)(2,1)} %collective-permute-done.23.refs_0_, bf16[1024,2048]{1,0:T(8,128)(2,1)} %all-gather.5.cloned.1.call-done.refs_1_, s32[5]{0:T(128)} %stack.158.refs_0_.refs_9_.refs_10_.refs_2_, ...), custom_call_target="tpu_custom_call" | custom-call | tf_op jit(solution)/shard_map/term_blocks/pallas_call | solution.py:59
  188.4 7.6 %collective-permute-done.16 = bf16[2,768,128]{2,1,0:T(8,128)(2,1)S(1)} collective-permute-done((bf16[2,768,128]{2,1,0:T(8,128)(2,1)S(1)}, bf16[2,768,128]{2,1,0:T(8,128)(2,1)S(1)}, u32[]{:S(2)}, u32[]{:S(2)}) %collective-permute-start.16) | collective-permute-done | bytes 393248 | tf_op jit(solution)/shard_map/ppermute | solution.py:25
  196.0 8.1 %collective-permute-done.17 = bf16[2,768,128]{2,1,0:T(8,128)(2,1)S(1)} collective-permute-done((bf16[2,768,128]{2,1,0:T(8,128)(2,1)S(1)}, bf16[2,768,128]{2,1,0:T(8,128)(2,1)S(1)}, u32[]{:S(2)}, u32[]{:S(2)}) %collective-permute-start.17) | collective-permute-done | bytes 393248 | tf_op jit(solution)/shard_map/ppermute | solution.py:25
  205.8 4.6 %all-to-all-start.1 = ((bf16[4,2,768,128]{3,2,1,0:T(8,128)(2,1)}), bf16[4,2,768,128]{3,2,1,0:T(8,128)(2,1)S(1)}, u32[]{:S(2)}, u32[]{:S(2)}) async-start(bf16[4,2,768,128]{3,2,1,0:T(8,128)(2,1)} %gate.7), calls=%async_computation.1 | async-start | bytes 3145728 | tf_op jit(solution)/shard_map/all_to_all | solution.py:391
  210.5 5.2 %collective-permute-start.21 = (bf16[1024,128]{1,0:T(8,128)(2,1)S(1)}, bf16[1024,128]{1,0:T(8,128)(2,1)S(1)}, u32[]{:S(2)}, u32[]{:S(2)}) collective-permute-start(bf16[1024,128]{1,0:T(8,128)(2,1)S(1)} %copy-done.15), channel_id=1, source_target_pairs={{0,0},{4,132},{64,64},{68,196},{1,1},{5,133},{65,65},{69,197},{2,2... | collective-permute-start | bytes 786440 | tf_op jit(solution)/shard_map/ppermute | solution.py:35
  218.3 11.6 %all-to-all-done.1 = bf16[4,2,768,128]{3,2,1,0:T(8,128)(2,1)S(1)} async-done(((bf16[4,2,768,128]{3,2,1,0:T(8,128)(2,1)}), bf16[4,2,768,128]{3,2,1,0:T(8,128)(2,1)S(1)}, u32[]{:S(2)}, u32[]{:S(2)}) %all-to-all-start.1) | async-done | bytes 1572896 | tf_op jit(solution)/shard_map/all_to_all | solution.py:391
  232.3 5.1 %collective-permute-start.27 = (bf16[1024,128]{1,0:T(8,128)(2,1)}, bf16[1024,128]{1,0:T(8,128)(2,1)S(1)}, u32[]{:S(2)}, u32[]{:S(2)}) collective-permute-start(bf16[1024,128]{1,0:T(8,128)(2,1)} %gate.9), channel_id=1, source_target_pairs={{0,4},{4,128},{64,68},{68,192},{1,5},{5,129},{65,69},{69,193},{2,6... | collective-permute-start | bytes 786440 | tf_op jit(solution)/shard_map/ppermute | solution.py:35
  240.8 6.7 %collective-permute-start.25 = (bf16[1024,128]{1,0:T(8,128)(2,1)}, bf16[1024,128]{1,0:T(8,128)(2,1)S(1)}, u32[]{:S(2)}, u32[]{:S(2)}) collective-permute-start(bf16[1024,128]{1,0:T(8,128)(2,1)} %gate.8), channel_id=1, source_target_pairs={{0,68},{4,192},{64,4},{68,128},{1,69},{5,193},{65,5},{69,129},{2,7... | collective-permute-start | bytes 786440 | tf_op jit(solution)/shard_map/ppermute | solution.py:35
  248.8 6.5 %collective-permute-done.27.refs_6_ = bf16[1024,128]{1,0:T(8,128)(2,1)S(1)} collective-permute-done((bf16[1024,128]{1,0:T(8,128)(2,1)}, bf16[1024,128]{1,0:T(8,128)(2,1)S(1)}, u32[]{:S(2)}, u32[]{:S(2)}) %collective-permute-start.27) | collective-permute-done | bytes 262176 | tf_op jit(solution)/shard_map/ppermute | solution.py:35
  255.3 4.3 %collective-permute-done.26.refs_5_ = bf16[1024,128]{1,0:T(8,128)(2,1)S(1)} collective-permute-done((bf16[1024,128]{1,0:T(8,128)(2,1)}, bf16[1024,128]{1,0:T(8,128)(2,1)S(1)}, u32[]{:S(2)}, u32[]{:S(2)}) %collective-permute-start.26) | collective-permute-done | bytes 262176 | tf_op jit(solution)/shard_map/ppermute | solution.py:35
  260.4 2.5 finish.1
  (124 shorter events, 50.3 us)
Async XLA Ops:
  7.2 96.2 %all-gather.3.cloned.1.call-start = ((), (), s32[]{:S(2)}) async-start(), calls=%async_computation.2 | async-start | bytes 2162688 | tf_op jit(solution)/shard_map/all_gather | solution.py:265
  7.2 9.4 %collective-permute-start.7 = (bf16[256,128]{1,0:T(8,128)(2,1)}, bf16[256,128]{1,0:T(8,128)(2,1)S(1)}, u32[]{:S(2)}, u32[]{:S(2)}) collective-permute-start(bf16[256,128]{1,0:T(8,128)(2,1)} %param.14), channel_id=1, source_target_pairs={{0,0},{4,128},{64,64},{68,192},{128,4},{132,132},{192,68},{196,196... | collective-permute-start | bytes 196616 | tf_op jit(solution)/shard_map/ppermute | solution.py:35
  25.4 36.0 %all-to-all-start = ((bf16[8,144,768]{2,1,0:T(8,128)(2,1)}), bf16[8,144,768]{2,1,0:T(8,128)(2,1)S(1)}, u32[]{:S(2)}, u32[]{:S(2)}) async-start(bf16[8,144,768]{2,1,0:T(8,128)(2,1)} %pack.1), calls=%async_computation | async-start | bytes 3538944 | tf_op jit(solution)/shard_map/all_to_all | solution.py:305
  31.3 127.9 %all-gather.5.cloned.1.call-start = ((), (), s32[]{:S(2)}) async-start(), calls=%async_computation.3 | async-start | bytes 5242880 | tf_op jit(solution)/shard_map/all_gather | solution.py:330
  31.3 41.5 %collective-permute-start = (bf16[128,2048]{1,0:T(8,128)(2,1)S(1)}, bf16[128,2048]{1,0:T(8,128)(2,1)S(1)}, u32[]{:S(2)}, u32[]{:S(2)}) collective-permute-start(bf16[128,2048]{1,0:T(8,128)(2,1)S(1)} %copy-done.2), channel_id=1, source_target_pairs={{1,0},{2,1},{3,2},{0,3},{5,4},{6,5},{7,6},{4,7},{9,8},{10,9},{11,1... | collective-permute-start | bytes 1572872 | tf_op jit(solution)/shard_map/ppermute | solution.py:25
  34.0 39.4 %collective-permute-start.1 = (bf16[128,2048]{1,0:T(8,128)(2,1)S(1)}, bf16[128,2048]{1,0:T(8,128)(2,1)S(1)}, u32[]{:S(2)}, u32[]{:S(2)}) collective-permute-start(bf16[128,2048]{1,0:T(8,128)(2,1)S(1)} %copy-done.2), channel_id=1, source_target_pairs={{2,0},{3,1},{0,2},{1,3},{6,4},{7,5},{4,6},{5,7},{10,8},{11,9},{8,1... | collective-permute-start | bytes 1572872 | tf_op jit(solution)/shard_map/ppermute | solution.py:25
  34.9 39.8 %collective-permute-start.2 = (bf16[128,2048]{1,0:T(8,128)(2,1)S(1)}, bf16[128,2048]{1,0:T(8,128)(2,1)}, u32[]{:S(2)}, u32[]{:S(2)}) collective-permute-start(bf16[128,2048]{1,0:T(8,128)(2,1)S(1)} %copy-done.2), channel_id=1, source_target_pairs={{3,0},{0,1},{1,2},{2,3},{7,4},{4,5},{5,6},{6,7},{11,8},{8,9},{9,10... | collective-permute-start | bytes 1572872 | tf_op jit(solution)/shard_map/ppermute | solution.py:25
  35.7 38.9 %collective-permute-start.3 = (bf16[128,2048]{1,0:T(8,128)(2,1)}, bf16[128,2048]{1,0:T(8,128)(2,1)}, u32[]{:S(2)}, u32[]{:S(2)}) collective-permute-start(bf16[128,2048]{1,0:T(8,128)(2,1)} %get-tuple-element.20), channel_id=1, source_target_pairs={{4,0},{0,4},{5,1},{1,5},{6,2},{2,6},{7,3},{3,7},{12,8},{8,12},{13,... | collective-permute-start | bytes 1572872 | tf_op jit(solution)/shard_map/ppermute | solution.py:25
  39.5 45.7 %collective-permute-start.8 = (bf16[128,2048]{1,0:T(8,128)(2,1)}, bf16[128,2048]{1,0:T(8,128)(2,1)}, u32[]{:S(2)}, u32[]{:S(2)}) collective-permute-start(bf16[128,2048]{1,0:T(8,128)(2,1)} %get-tuple-element.22), channel_id=1, source_target_pairs={{4,0},{0,4},{5,1},{1,5},{6,2},{2,6},{7,3},{3,7},{12,8},{8,12},{13,... | collective-permute-start | bytes 1572872 | tf_op jit(solution)/shard_map/ppermute | solution.py:25
  72.8 21.1 %collective-permute-start.9 = (bf16[256,1024]{1,0:T(8,128)(2,1)}, bf16[256,1024]{1,0:T(8,128)(2,1)S(1)}, u32[]{:S(2)}, u32[]{:S(2)}) collective-permute-start(bf16[256,1024]{1,0:T(8,128)(2,1)} %get-tuple-element.23.refs_8_), channel_id=1, source_target_pairs={{4,0},{0,4},{5,1},{1,5},{6,2},{2,6},{7,3},{3,7},{12,8},{8,12},{13,... | collective-permute-start | bytes 1572872 | tf_op jit(solution)/shard_map/ppermute | solution.py:25
  74.7 25.2 %collective-permute-start.4 = (bf16[128,2048]{1,0:T(8,128)(2,1)}, bf16[128,2048]{1,0:T(8,128)(2,1)S(1)}, u32[]{:S(2)}, u32[]{:S(2)}) collective-permute-start(bf16[128,2048]{1,0:T(8,128)(2,1)} %gate.5.refs_4_), channel_id=1, source_target_pairs={{1,0},{2,1},{3,2},{0,3},{5,4},{6,5},{7,6},{4,7},{9,8},{10,9},{11,1... | collective-permute-start | bytes 1572872 | tf_op jit(solution)/shard_map/ppermute | solution.py:25
  76.8 23.1 %collective-permute-start.5 = (bf16[128,2048]{1,0:T(8,128)(2,1)}, bf16[128,2048]{1,0:T(8,128)(2,1)S(1)}, u32[]{:S(2)}, u32[]{:S(2)}) collective-permute-start(bf16[128,2048]{1,0:T(8,128)(2,1)} %gate.5.refs_4_), channel_id=1, source_target_pairs={{2,0},{3,1},{0,2},{1,3},{6,4},{7,5},{4,6},{5,7},{10,8},{11,9},{8,1... | collective-permute-start | bytes 1572872 | tf_op jit(solution)/shard_map/ppermute | solution.py:25
  78.3 25.2 %collective-permute-start.6 = (bf16[128,2048]{1,0:T(8,128)(2,1)}, bf16[128,2048]{1,0:T(8,128)(2,1)S(1)}, u32[]{:S(2)}, u32[]{:S(2)}) collective-permute-start(bf16[128,2048]{1,0:T(8,128)(2,1)} %gate.5.refs_4_), channel_id=1, source_target_pairs={{3,0},{0,1},{1,2},{2,3},{7,4},{4,5},{5,6},{6,7},{11,8},{8,9},{9,10... | collective-permute-start | bytes 1572872 | tf_op jit(solution)/shard_map/ppermute | solution.py:25
  112.9 14.1 %collective-permute-start.10 = (bf16[1024,256]{1,0:T(8,128)(2,1)}, bf16[1024,256]{1,0:T(8,128)(2,1)S(1)}, u32[]{:S(2)}, u32[]{:S(2)}) collective-permute-start(bf16[1024,256]{1,0:T(8,128)(2,1)} %get-tuple-element.25.refs_11_), channel_id=1, source_target_pairs={{4,0},{0,4},{5,1},{1,5},{6,2},{2,6},{7,3},{3,7},{12,8},{8,12},{13,... | collective-permute-start | bytes 1572872 | tf_op jit(solution)/shard_map/ppermute | solution.py:25
  137.4 35.7 %collective-permute-start.23 = (bf16[768,1024]{1,0:T(8,128)(2,1)S(1)}, bf16[768,1024]{1,0:T(8,128)(2,1)}, u32[]{:S(2)}, u32[]{:S(2)}) collective-permute-start(bf16[768,1024]{1,0:T(8,128)(2,1)S(1)} %copy-done.1), channel_id=1, source_target_pairs={{4,0},{0,4},{5,1},{1,5},{6,2},{2,6},{7,3},{3,7},{12,8},{8,12},{13,... | collective-permute-start | bytes 4718600 | tf_op jit(solution)/shard_map/ppermute | solution.py:25
  141.7 10.8 %collective-permute-start.12 = (bf16[2,512,128]{2,1,0:T(8,128)(2,1)S(1)}, bf16[2,512,128]{2,1,0:T(8,128)(2,1)S(1)}, u32[]{:S(2)}, u32[]{:S(2)}) collective-permute-start(bf16[2,512,128]{2,1,0:T(8,128)(2,1)S(1)} %get-tuple-element.37), channel_id=1, source_target_pairs={{32,0},{48,16},{0,32},{16,48},{33,1},{49,17},{1,33},{17,49},{34,2}... | collective-permute-start | bytes 786440 | tf_op jit(solution)/shard_map/ppermute | solution.py:25
  144.0 13.4 %collective-permute-start.13 = (bf16[2,512,128]{2,1,0:T(8,128)(2,1)S(1)}, bf16[2,512,128]{2,1,0:T(8,128)(2,1)S(1)}, u32[]{:S(2)}, u32[]{:S(2)}) collective-permute-start(bf16[2,512,128]{2,1,0:T(8,128)(2,1)S(1)} %get-tuple-element.39), channel_id=1, source_target_pairs={{48,0},{0,16},{16,32},{32,48},{49,1},{1,17},{17,33},{33,49},{50,2}... | collective-permute-start | bytes 786440 | tf_op jit(solution)/shard_map/ppermute | solution.py:25
  144.0 13.4 %collective-permute-start.14 = (bf16[2,512,128]{2,1,0:T(8,128)(2,1)S(1)}, bf16[2,512,128]{2,1,0:T(8,128)(2,1)S(1)}, u32[]{:S(2)}, u32[]{:S(2)}) collective-permute-start(bf16[2,512,128]{2,1,0:T(8,128)(2,1)S(1)} %get-tuple-element.38), channel_id=1, source_target_pairs={{16,0},{32,16},{48,32},{0,48},{17,1},{33,17},{49,33},{1,49},{18,2}... | collective-permute-start | bytes 786440 | tf_op jit(solution)/shard_map/ppermute | solution.py:25
  166.4 14.1 %collective-permute-start.15 = (bf16[4,2,768,128]{3,2,1,0:T(8,128)(2,1)}, bf16[4,2,768,128]{3,2,1,0:T(8,128)(2,1)}, u32[]{:S(2)}, u32[]{:S(2)}) collective-permute-start(bf16[4,2,768,128]{3,2,1,0:T(8,128)(2,1)} %get-tuple-element.29), channel_id=1, source_target_pairs={{8,0},{0,8},{9,1},{1,9},{10,2},{2,10},{11,3},{3,11},{12,4},{4,12},... | collective-permute-start | bytes 4718600 | tf_op jit(solution)/shard_map/ppermute | solution.py:25
  180.5 6.3 %collective-permute-start.24 = (bf16[4,2,768,128]{3,2,1,0:T(8,128)(2,1)}, bf16[4,2,768,128]{3,2,1,0:T(8,128)(2,1)S(1)}, u32[]{:S(2)}, u32[]{:S(2)}) collective-permute-start(bf16[4,2,768,128]{3,2,1,0:T(8,128)(2,1)} %get-tuple-element.31), channel_id=1, source_target_pairs={{8,0},{0,8},{9,1},{1,9},{10,2},{2,10},{11,3},{3,11},{12,4},{4,12},... | collective-permute-start | bytes 4718600 | tf_op jit(solution)/shard_map/ppermute | solution.py:25
  182.4 13.5 %collective-permute-start.16 = (bf16[2,768,128]{2,1,0:T(8,128)(2,1)S(1)}, bf16[2,768,128]{2,1,0:T(8,128)(2,1)S(1)}, u32[]{:S(2)}, u32[]{:S(2)}) collective-permute-start(bf16[2,768,128]{2,1,0:T(8,128)(2,1)S(1)} %get-tuple-element.34), channel_id=1, source_target_pairs={{32,0},{48,16},{0,32},{16,48},{33,1},{49,17},{1,33},{17,49},{34,2}... | collective-permute-start | bytes 1179656 | tf_op jit(solution)/shard_map/ppermute | solution.py:25
  184.7 19.4 %collective-permute-start.17 = (bf16[2,768,128]{2,1,0:T(8,128)(2,1)S(1)}, bf16[2,768,128]{2,1,0:T(8,128)(2,1)S(1)}, u32[]{:S(2)}, u32[]{:S(2)}) collective-permute-start(bf16[2,768,128]{2,1,0:T(8,128)(2,1)S(1)} %get-tuple-element.36), channel_id=1, source_target_pairs={{48,0},{0,16},{16,32},{32,48},{49,1},{1,17},{17,33},{33,49},{50,2}... | collective-permute-start | bytes 1179656 | tf_op jit(solution)/shard_map/ppermute | solution.py:25
  184.8 19.4 %collective-permute-start.18 = (bf16[2,768,128]{2,1,0:T(8,128)(2,1)S(1)}, bf16[2,768,128]{2,1,0:T(8,128)(2,1)S(1)}, u32[]{:S(2)}, u32[]{:S(2)}) collective-permute-start(bf16[2,768,128]{2,1,0:T(8,128)(2,1)S(1)} %get-tuple-element.35), channel_id=1, source_target_pairs={{16,0},{32,16},{48,32},{0,48},{17,1},{33,17},{49,33},{1,49},{18,2}... | collective-permute-start | bytes 1179656 | tf_op jit(solution)/shard_map/ppermute | solution.py:25
  205.8 24.1 %all-to-all-start.1 = ((bf16[4,2,768,128]{3,2,1,0:T(8,128)(2,1)}), bf16[4,2,768,128]{3,2,1,0:T(8,128)(2,1)S(1)}, u32[]{:S(2)}, u32[]{:S(2)}) async-start(bf16[4,2,768,128]{3,2,1,0:T(8,128)(2,1)} %gate.7), calls=%async_computation.1 | async-start | bytes 3145728 | tf_op jit(solution)/shard_map/all_to_all | solution.py:391
  210.5 20.4 %collective-permute-start.21 = (bf16[1024,128]{1,0:T(8,128)(2,1)S(1)}, bf16[1024,128]{1,0:T(8,128)(2,1)S(1)}, u32[]{:S(2)}, u32[]{:S(2)}) collective-permute-start(bf16[1024,128]{1,0:T(8,128)(2,1)S(1)} %copy-done.15), channel_id=1, source_target_pairs={{0,0},{4,132},{64,64},{68,196},{1,1},{5,133},{65,65},{69,197},{2,2... | collective-permute-start | bytes 786440 | tf_op jit(solution)/shard_map/ppermute | solution.py:35
  215.6 15.2 %collective-permute-start.22 = (bf16[1024,128]{1,0:T(8,128)(2,1)S(1)}, bf16[1024,128]{1,0:T(8,128)(2,1)S(1)}, u32[]{:S(2)}, u32[]{:S(2)}) collective-permute-start(bf16[1024,128]{1,0:T(8,128)(2,1)S(1)} %copy-done.15), channel_id=1, source_target_pairs={{128,0},{132,132},{192,64},{196,196},{129,1},{133,133},{193,65},{1... | collective-permute-start | bytes 786440 | tf_op jit(solution)/shard_map/ppermute | solution.py:35
  216.3 23.0 %collective-permute-start.19 = (bf16[1024,128]{1,0:T(8,128)(2,1)S(1)}, bf16[1024,128]{1,0:T(8,128)(2,1)S(1)}, u32[]{:S(2)}, u32[]{:S(2)}) collective-permute-start(bf16[1024,128]{1,0:T(8,128)(2,1)S(1)} %copy-done.14), channel_id=1, source_target_pairs={{0,64},{4,196},{64,0},{68,132},{1,65},{5,197},{65,1},{69,133},{2,6... | collective-permute-start | bytes 786440 | tf_op jit(solution)/shard_map/ppermute | solution.py:35
  217.7 21.7 %collective-permute-start.20 = (bf16[1024,128]{1,0:T(8,128)(2,1)S(1)}, bf16[1024,128]{1,0:T(8,128)(2,1)S(1)}, u32[]{:S(2)}, u32[]{:S(2)}) collective-permute-start(bf16[1024,128]{1,0:T(8,128)(2,1)S(1)} %copy-done.14), channel_id=1, source_target_pairs={{128,64},{132,196},{192,0},{196,132},{129,65},{133,197},{193,1},{1... | collective-permute-start | bytes 786440 | tf_op jit(solution)/shard_map/ppermute | solution.py:35
  232.3 23.1 %collective-permute-start.27 = (bf16[1024,128]{1,0:T(8,128)(2,1)}, bf16[1024,128]{1,0:T(8,128)(2,1)S(1)}, u32[]{:S(2)}, u32[]{:S(2)}) collective-permute-start(bf16[1024,128]{1,0:T(8,128)(2,1)} %gate.9), channel_id=1, source_target_pairs={{0,4},{4,128},{64,68},{68,192},{1,5},{5,129},{65,69},{69,193},{2,6... | collective-permute-start | bytes 786440 | tf_op jit(solution)/shard_map/ppermute | solution.py:35
  237.3 18.0 %collective-permute-start.28 = (bf16[1024,128]{1,0:T(8,128)(2,1)}, bf16[1024,128]{1,0:T(8,128)(2,1)S(1)}, u32[]{:S(2)}, u32[]{:S(2)}) collective-permute-start(bf16[1024,128]{1,0:T(8,128)(2,1)} %gate.9), channel_id=1, source_target_pairs={{128,4},{132,128},{192,68},{196,192},{129,5},{133,129},{193,69},{1... | collective-permute-start | bytes 786440 | tf_op jit(solution)/shard_map/ppermute | solution.py:35
  240.8 14.6 %collective-permute-start.25 = (bf16[1024,128]{1,0:T(8,128)(2,1)}, bf16[1024,128]{1,0:T(8,128)(2,1)S(1)}, u32[]{:S(2)}, u32[]{:S(2)}) collective-permute-start(bf16[1024,128]{1,0:T(8,128)(2,1)} %gate.8), channel_id=1, source_target_pairs={{0,68},{4,192},{64,4},{68,128},{1,69},{5,193},{65,5},{69,129},{2,7... | collective-permute-start | bytes 786440 | tf_op jit(solution)/shard_map/ppermute | solution.py:35
  247.5 12.2 %collective-permute-start.26 = (bf16[1024,128]{1,0:T(8,128)(2,1)}, bf16[1024,128]{1,0:T(8,128)(2,1)S(1)}, u32[]{:S(2)}, u32[]{:S(2)}) collective-permute-start(bf16[1024,128]{1,0:T(8,128)(2,1)} %gate.8), channel_id=1, source_target_pairs={{128,68},{132,192},{192,4},{196,128},{129,69},{133,193},{193,5},{1... | collective-permute-start | bytes 786440 | tf_op jit(solution)/shard_map/ppermute | solution.py:35
  (27 other events, 98.9 us)
Sparse Core Ops, SparseCore 0:
  17.4 59.4 all-gather.2
  106.6 50.0 all-gather.4

commit v3 on v2

--- a/solution.py
+++ b/solution.py
@@ -275,6 +275,17 @@
     )
     scaled_pair = recv(scaled_send, "l", 1)
     scaled = ring(scaled_keep)
+
+    to_heads = call(
+        pack_kernel,
+        "pack",
+        [queries, key_rows, value_rows, segment_ids],
+        [VMEM] * 4,
+        shape(8, TOK + 16, 768),
+        VMEM,
+        deps=[scaled_keep],
+    )
+    packed = lax.all_to_all(to_heads, SEQ, split_axis=0, concat_axis=0, tiled=True)
     order = [
         ((half * 2 + (h + a) % 2) * 4 + at_y) * 2 + (c + dc) % 2
         for half in (l, 1 - l)
@@ -289,20 +300,9 @@
         [SMEM, VMEM],
         (shape(TOK, HALF),) * 2,
         (VMEM,) * 2,
-        deps=[scaled_keep],
+        deps=[packed],
     )
     layer_pair = recv(layer_send, "l", 1)
-
-    to_heads = call(
-        pack_kernel,
-        "pack",
-        [queries, key_rows, value_rows, segment_ids],
-        [VMEM] * 4,
-        shape(8, TOK + 16, 768),
-        VMEM,
-        deps=[scaled_keep],
-    )
-    packed = lax.all_to_all(to_heads, SEQ, split_axis=0, concat_axis=0, tiled=True)
     scaled = scaled + ring(gate(scaled_pair, [packed] + scaled[1:]))
 
     attended, probs = call(

time: 273 us -> 273 us (level)
    all_to_all x1, waiting for transfers between devices: 19.7 us -> 23.9 us  [shards(): lax.all_to_all(to_heads, SEQ, split_axis=0, concat_axis=0, tiled=True)]
    ppermute x20, waiting for transfers between devices: 69.3 us -> 66.1 us  [recv(): return lax.ppermute(block, axis, [((i + offset) % n, i) for i in range(n)])]
    unnamed x52 -> x54, local copies, waits for them, and re-layouts: 8.47 us -> 9.39 us
  transfers between devices with their start and end apart: 33 -> 33, of which waited for: 17 -> 16; matrix products, arithmetic and copies ran while one was open for 5% -> 5% of each run, Pallas kernels for 20% -> 20%
where the time goes in v3:
time: 273 us; the launch traced here: 270 us
  waiting for transfers between devices  116 us (42%)
  Pallas kernels  58.2 us (21%)
  starting transfers between devices  56.9 us (21%)
  between operations  15.1 us (6%)
  local copies, waits for them, and re-layouts  12.2 us (4%)
  other arithmetic  11.6 us (4%)
    ppermute x20, waiting for transfers between devices, recv(): return lax.ppermute(block, axis, [((i + offset) % n, i) for i in range(n)])  66.1 us
    pallas_call x11, Pallas kernels, call(): pl.pallas_call(body, grid=grid, out_shape=outs, in_specs=[whole(s, a) for...  58.2 us
    ppermute x9, starting transfers between devices, send_zz(): return lax.ppermute(block, ('h', 'l'), pairs)  28.1 us
    all_to_all x1, waiting for transfers between devices, shards(): lax.all_to_all(to_heads, SEQ, split_axis=0, concat_axis=0, tiled=True)  23.9 us
    ppermute x20, starting transfers between devices, recv(): return lax.ppermute(block, axis, [((i + offset) % n, i) for i in range(n)])  18.3 us
    ppermute x9, waiting for transfers between devices, send_zz(): return lax.ppermute(block, ('h', 'l'), pairs)  14.3 us
    all_to_all x1, waiting for transfers between devices, shards(): lax.all_to_all(blocks, 'y', split_axis=0, concat_axis=0, tiled=True)  11.5 us
    unnamed x54, local copies, waits for them, and re-layouts  9.39 us
  transfers between devices with their start and end apart: 33, of which 16 were waited for; matrix products, arithmetic and copies ran while one was open for 5% of the time, Pallas kernels for 20%

profile of v3, /device:TPU:104, one launch (start us, length us, event | category | flops | bytes accessed | tf_op | source)
XLA Modules:
  0.0 269.8 jit_solution(9244822616068981242)
XLA Ops:
  7.2 5.9 %collective-permute-start.7 = (bf16[256,128]{1,0:T(8,128)(2,1)}, bf16[256,128]{1,0:T(8,128)(2,1)S(1)}, u32[]{:S(2)}, u32[]{:S(2)}) collective-permute-start(bf16[256,128]{1,0:T(8,128)(2,1)} %param.14), channel_id=1, source_target_pairs={{0,0},{4,128},{64,64},{68,192},{128,4},{132,132},{192,68},{196,196... | collective-permute-start | bytes 196616 | tf_op jit(solution)/shard_map/ppermute | solution.py:35
  13.2 3.4 %collective-permute-done.7 = bf16[256,128]{1,0:T(8,128)(2,1)S(1)} collective-permute-done((bf16[256,128]{1,0:T(8,128)(2,1)}, bf16[256,128]{1,0:T(8,128)(2,1)S(1)}, u32[]{:S(2)}, u32[]{:S(2)}) %collective-permute-start.7) | collective-permute-done | bytes 65568 | tf_op jit(solution)/shard_map/ppermute | solution.py:35
  20.0 2.5 scale.1
  22.4 2.9 %pack.1 = bf16[8,144,768]{2,1,0:T(8,128)(2,1)} custom-call(bf16[128,2048]{1,0:T(8,128)(2,1)} %refs_0_.1, bf16[128,2048]{1,0:T(8,128)(2,1)} %refs_1_.4, bf16[128,2048]{1,0:T(8,128)(2,1)} %refs_2_.1, s32[1,128]{1,0:T(1,128)} %refs_3_.1, bf16[128,2048]{1,0:T(8,128)(2,1)} %get-tuple-element.18.refs_4_.refs_0_), custom_call_target="tpu_custom_call" | custom-call | tf_op jit(solution)/shard_map/pack/pallas_call | solution.py:59
  25.3 5.8 %all-to-all-start = ((bf16[8,144,768]{2,1,0:T(8,128)(2,1)}), bf16[8,144,768]{2,1,0:T(8,128)(2,1)S(1)}, u32[]{:S(2)}, u32[]{:S(2)}) async-start(bf16[8,144,768]{2,1,0:T(8,128)(2,1)} %pack.1), calls=%async_computation | async-start | bytes 3538944 | tf_op jit(solution)/shard_map/all_to_all | solution.py:288
  31.1 2.7 collective-permute-start
  37.3 23.9 %all-to-all-done.refs_1_.refs_2_ = bf16[8,144,768]{2,1,0:T(8,128)(2,1)S(1)} async-done(((bf16[8,144,768]{2,1,0:T(8,128)(2,1)}), bf16[8,144,768]{2,1,0:T(8,128)(2,1)S(1)}, u32[]{:S(2)}, u32[]{:S(2)}) %all-to-all-start) | async-done | bytes 1769504 | tf_op jit(solution)/shard_map/all_to_all | solution.py:288
  62.5 2.5 reorder.1
  65.4 10.2 %attention_forward.1 = (bf16[256,1024]{1,0:T(8,128)(2,1)}, bf16[2,1024,1024]{2,1,0:T(8,128)(2,1)}) custom-call(s32[8]{0:T(128)} %stack.152.refs_0_, bf16[8,144,768]{2,1,0:T(8,128)(2,1)} %copy-done), custom_call_target="tpu_custom_call" | custom-call | tf_op jit(solution)/shard_map/attention_forward/pallas_call | solution.py:59
  80.3 4.6 %collective-permute-done.8.refs_1_ = bf16[128,2048]{1,0:T(8,128)(2,1)S(1)} collective-permute-done((bf16[128,2048]{1,0:T(8,128)(2,1)}, bf16[128,2048]{1,0:T(8,128)(2,1)S(1)}, u32[]{:S(2)}, u32[]{:S(2)}) %collective-permute-start.8) | collective-permute-done | bytes 524320 | tf_op jit(solution)/shard_map/ppermute | solution.py:25
  84.9 8.9 %collective-permute-done.9.refs_2_.refs_9_ = bf16[256,1024]{1,0:T(8,128)(2,1)S(1)} collective-permute-done((bf16[256,1024]{1,0:T(8,128)(2,1)}, bf16[256,1024]{1,0:T(8,128)(2,1)S(1)}, u32[]{:S(2)}, u32[]{:S(2)}) %collective-permute-start.9) | collective-permute-done | bytes 524320 | tf_op jit(solution)/shard_map/ppermute | solution.py:25
  93.8 6.1 %collective-permute-done.4.refs_4_.refs_5_ = bf16[128,2048]{1,0:T(8,128)(2,1)S(1)} collective-permute-done((bf16[128,2048]{1,0:T(8,128)(2,1)}, bf16[128,2048]{1,0:T(8,128)(2,1)S(1)}, u32[]{:S(2)}, u32[]{:S(2)}) %collective-permute-start.4) | collective-permute-done | bytes 524320 | tf_op jit(solution)/shard_map/ppermute | solution.py:25
  99.9 3.6 %collective-permute-done.6.refs_6_.refs_7_ = bf16[128,2048]{1,0:T(8,128)(2,1)S(1)} collective-permute-done((bf16[128,2048]{1,0:T(8,128)(2,1)}, bf16[128,2048]{1,0:T(8,128)(2,1)S(1)}, u32[]{:S(2)}, u32[]{:S(2)}) %collective-permute-start.6) | collective-permute-done | bytes 524320 | tf_op jit(solution)/shard_map/ppermute | solution.py:25
  106.5 6.4 %dout.1 = (f32[1024,256]{1,0:T(8,128)}, bf16[1024,256]{1,0:T(8,128)(2,1)}) custom-call(bf16[128,2048]{1,0:T(8,128)(2,1)} %get-tuple-element.18.refs_4_.refs_0_, bf16[128,2048]{1,0:T(8,128)(2,1)} %copy-done.3, bf16[128,2048]{1,0:T(8,128)(2,1)} %copy-done.4, bf16[128,2048]{1,0:T(8,128)(2,1)} %copy-done.5, bf16[128,2048]{1,0:T(8,128)(2,1)} %gate.5.refs_4_, ...), custom_call_target="tpu_custom_call" | custom-call | tf_op jit(solution)/shard_map/dout/pallas_call | solution.py:59
  113.0 6.2 %out_terms.1 = (bf16[4,2,512,128]{3,2,1,0:T(8,128)(2,1)}, bf16[4,2,512,128]{3,2,1,0:T(8,128)(2,1)}) custom-call(bf16[128,2048]{1,0:T(8,128)(2,1)} %get-tuple-element.18.refs_4_.refs_0_, bf16[128,2048]{1,0:T(8,128)(2,1)} %copy-done.3, bf16[128,2048]{1,0:T(8,128)(2,1)} %copy-done.4, bf16[128,2048]{1,0:T(8,128)(2,1)} %copy-done.5, ...), custom_call_target="tpu_custom_call" | custom-call | tf_op jit(solution)/shard_map/out_terms/pallas_call | solution.py:59
  119.2 7.8 %collective-permute-done.10 = bf16[1024,256]{1,0:T(8,128)(2,1)S(1)} collective-permute-done((bf16[1024,256]{1,0:T(8,128)(2,1)}, bf16[1024,256]{1,0:T(8,128)(2,1)S(1)}, u32[]{:S(2)}, u32[]{:S(2)}) %collective-permute-start.10) | collective-permute-done | bytes 524320 | tf_op jit(solution)/shard_map/ppermute | solution.py:25
  127.9 8.1 %attention_backward.1.refs_1_.refs_0_ = bf16[768,1024]{1,0:T(8,128)(2,1)} custom-call(s32[8]{0:T(128)} %stack.152.refs_0_, bf16[8,144,768]{2,1,0:T(8,128)(2,1)} %copy-done, bf16[2,1024,1024]{2,1,0:T(8,128)(2,1)} %get-tuple-element.19.refs_2_, bf16[1024,256]{1,0:T(8,128)(2,1)} %add_convert_fusion.3.refs_3_, bf16[4,2,512,128]{3,2,1,0:T(8,128)(2,1)} %get-tuple-element.26.refs_4_), custom_call_target="tpu_custom_call" | custom-call | tf_op jit(solution)/shard_map/attention_backward/pallas_call | solution.py:59
  146.1 6.4 %collective-permute-done.12 = bf16[2,512,128]{2,1,0:T(8,128)(2,1)S(1)} collective-permute-done((bf16[2,512,128]{2,1,0:T(8,128)(2,1)S(1)}, bf16[2,512,128]{2,1,0:T(8,128)(2,1)S(1)}, u32[]{:S(2)}, u32[]{:S(2)}) %collective-permute-start.12) | collective-permute-done | bytes 262176 | tf_op jit(solution)/shard_map/ppermute | solution.py:25
  152.4 4.9 %collective-permute-done.13 = bf16[2,512,128]{2,1,0:T(8,128)(2,1)S(1)} collective-permute-done((bf16[2,512,128]{2,1,0:T(8,128)(2,1)S(1)}, bf16[2,512,128]{2,1,0:T(8,128)(2,1)S(1)}, u32[]{:S(2)}, u32[]{:S(2)}) %collective-permute-start.13) | collective-permute-done | bytes 262176 | tf_op jit(solution)/shard_map/ppermute | solution.py:25
  159.2 7.2 %term_blocks.2 = (bf16[4,2,768,128]{3,2,1,0:T(8,128)(2,1)}, bf16[4,2,768,128]{3,2,1,0:T(8,128)(2,1)}) custom-call(bf16[768,1024]{1,0:T(8,128)(2,1)} %attention_backward.1.refs_1_.refs_0_, bf16[1024,2048]{1,0:T(8,128)(2,1)} %all-gather.5.cloned.1.call-done.refs_1_, s32[5]{0:T(128)} %stack.158.refs_0_.refs_9_.refs_10_.refs_2_, bf16[2,512,128]{2,1,0:T(8,128)(2,1)} %fusion.1.refs_3_), custom_call_target="tpu_custom_call" | custom-call | tf_op jit(solution)/shard_map/term_blocks/pallas_call | solution.py:59
  166.4 6.7 %collective-permute-done.23.refs_0_ = bf16[768,1024]{1,0:T(8,128)(2,1)} collective-permute-done((bf16[768,1024]{1,0:T(8,128)(2,1)S(1)}, bf16[768,1024]{1,0:T(8,128)(2,1)}, u32[]{:S(2)}, u32[]{:S(2)}) %collective-permute-start.23) | collective-permute-done | bytes 1572896 | tf_op jit(solution)/shard_map/ppermute | solution.py:25
  173.1 7.5 %term_blocks.3 = (bf16[4,2,768,128]{3,2,1,0:T(8,128)(2,1)}, bf16[4,2,768,128]{3,2,1,0:T(8,128)(2,1)}) custom-call(bf16[768,1024]{1,0:T(8,128)(2,1)} %collective-permute-done.23.refs_0_, bf16[1024,2048]{1,0:T(8,128)(2,1)} %all-gather.5.cloned.1.call-done.refs_1_, s32[5]{0:T(128)} %stack.158.refs_0_.refs_9_.refs_10_.refs_2_, ...), custom_call_target="tpu_custom_call" | custom-call | tf_op jit(solution)/shard_map/term_blocks/pallas_call | solution.py:59
  188.6 7.5 %collective-permute-done.16 = bf16[2,768,128]{2,1,0:T(8,128)(2,1)S(1)} collective-permute-done((bf16[2,768,128]{2,1,0:T(8,128)(2,1)S(1)}, bf16[2,768,128]{2,1,0:T(8,128)(2,1)S(1)}, u32[]{:S(2)}, u32[]{:S(2)}) %collective-permute-start.16) | collective-permute-done | bytes 393248 | tf_op jit(solution)/shard_map/ppermute | solution.py:25
  196.1 8.2 %collective-permute-done.17 = bf16[2,768,128]{2,1,0:T(8,128)(2,1)S(1)} collective-permute-done((bf16[2,768,128]{2,1,0:T(8,128)(2,1)S(1)}, bf16[2,768,128]{2,1,0:T(8,128)(2,1)S(1)}, u32[]{:S(2)}, u32[]{:S(2)}) %collective-permute-start.17) | collective-permute-done | bytes 393248 | tf_op jit(solution)/shard_map/ppermute | solution.py:25
  206.0 4.7 %all-to-all-start.1 = ((bf16[4,2,768,128]{3,2,1,0:T(8,128)(2,1)}), bf16[4,2,768,128]{3,2,1,0:T(8,128)(2,1)S(1)}, u32[]{:S(2)}, u32[]{:S(2)}) async-start(bf16[4,2,768,128]{3,2,1,0:T(8,128)(2,1)} %gate.7), calls=%async_computation.1 | async-start | bytes 3145728 | tf_op jit(solution)/shard_map/all_to_all | solution.py:391
  210.6 5.2 %collective-permute-start.21 = (bf16[1024,128]{1,0:T(8,128)(2,1)S(1)}, bf16[1024,128]{1,0:T(8,128)(2,1)S(1)}, u32[]{:S(2)}, u32[]{:S(2)}) collective-permute-start(bf16[1024,128]{1,0:T(8,128)(2,1)S(1)} %copy-done.15), channel_id=1, source_target_pairs={{0,0},{4,132},{64,64},{68,196},{1,1},{5,133},{65,65},{69,197},{2,2... | collective-permute-start | bytes 786440 | tf_op jit(solution)/shard_map/ppermute | solution.py:35
  218.6 11.5 %all-to-all-done.1 = bf16[4,2,768,128]{3,2,1,0:T(8,128)(2,1)S(1)} async-done(((bf16[4,2,768,128]{3,2,1,0:T(8,128)(2,1)}), bf16[4,2,768,128]{3,2,1,0:T(8,128)(2,1)S(1)}, u32[]{:S(2)}, u32[]{:S(2)}) %all-to-all-start.1) | async-done | bytes 1572896 | tf_op jit(solution)/shard_map/all_to_all | solution.py:391
  232.5 5.0 %collective-permute-start.27 = (bf16[1024,128]{1,0:T(8,128)(2,1)}, bf16[1024,128]{1,0:T(8,128)(2,1)S(1)}, u32[]{:S(2)}, u32[]{:S(2)}) collective-permute-start(bf16[1024,128]{1,0:T(8,128)(2,1)} %gate.9), channel_id=1, source_target_pairs={{0,4},{4,128},{64,68},{68,192},{1,5},{5,129},{65,69},{69,193},{2,6... | collective-permute-start | bytes 786440 | tf_op jit(solution)/shard_map/ppermute | solution.py:35
  240.9 6.7 %collective-permute-start.25 = (bf16[1024,128]{1,0:T(8,128)(2,1)}, bf16[1024,128]{1,0:T(8,128)(2,1)S(1)}, u32[]{:S(2)}, u32[]{:S(2)}) collective-permute-start(bf16[1024,128]{1,0:T(8,128)(2,1)} %gate.8), channel_id=1, source_target_pairs={{0,68},{4,192},{64,4},{68,128},{1,69},{5,193},{65,5},{69,129},{2,7... | collective-permute-start | bytes 786440 | tf_op jit(solution)/shard_map/ppermute | solution.py:35
  248.9 6.6 %collective-permute-done.27.refs_6_ = bf16[1024,128]{1,0:T(8,128)(2,1)S(1)} collective-permute-done((bf16[1024,128]{1,0:T(8,128)(2,1)}, bf16[1024,128]{1,0:T(8,128)(2,1)S(1)}, u32[]{:S(2)}, u32[]{:S(2)}) %collective-permute-start.27) | collective-permute-done | bytes 262176 | tf_op jit(solution)/shard_map/ppermute | solution.py:35
  255.5 4.3 %collective-permute-done.26.refs_5_ = bf16[1024,128]{1,0:T(8,128)(2,1)S(1)} collective-permute-done((bf16[1024,128]{1,0:T(8,128)(2,1)}, bf16[1024,128]{1,0:T(8,128)(2,1)S(1)}, u32[]{:S(2)}, u32[]{:S(2)}) %collective-permute-start.26) | collective-permute-done | bytes 262176 | tf_op jit(solution)/shard_map/ppermute | solution.py:35
  260.5 2.5 finish.1
  (126 shorter events, 48.4 us)
Async XLA Ops:
  7.2 96.3 %all-gather.3.cloned.1.call-start = ((), (), s32[]{:S(2)}) async-start(), calls=%async_computation.2 | async-start | bytes 2162688 | tf_op jit(solution)/shard_map/all_gather | solution.py:265
  7.2 9.4 %collective-permute-start.7 = (bf16[256,128]{1,0:T(8,128)(2,1)}, bf16[256,128]{1,0:T(8,128)(2,1)S(1)}, u32[]{:S(2)}, u32[]{:S(2)}) collective-permute-start(bf16[256,128]{1,0:T(8,128)(2,1)} %param.14), channel_id=1, source_target_pairs={{0,0},{4,128},{64,64},{68,192},{128,4},{132,132},{192,68},{196,196... | collective-permute-start | bytes 196616 | tf_op jit(solution)/shard_map/ppermute | solution.py:35
  25.3 35.9 %all-to-all-start = ((bf16[8,144,768]{2,1,0:T(8,128)(2,1)}), bf16[8,144,768]{2,1,0:T(8,128)(2,1)S(1)}, u32[]{:S(2)}, u32[]{:S(2)}) async-start(bf16[8,144,768]{2,1,0:T(8,128)(2,1)} %pack.1), calls=%async_computation | async-start | bytes 3538944 | tf_op jit(solution)/shard_map/all_to_all | solution.py:288
  31.1 128.1 %all-gather.5.cloned.1.call-start = ((), (), s32[]{:S(2)}) async-start(), calls=%async_computation.3 | async-start | bytes 5242880 | tf_op jit(solution)/shard_map/all_gather | solution.py:330
  31.1 44.5 %collective-permute-start = (bf16[128,2048]{1,0:T(8,128)(2,1)}, bf16[128,2048]{1,0:T(8,128)(2,1)S(1)}, u32[]{:S(2)}, u32[]{:S(2)}) collective-permute-start(bf16[128,2048]{1,0:T(8,128)(2,1)} %get-tuple-element.18.refs_4_.refs_0_), channel_id=1, source_target_pairs={{1,0},{2,1},{3,2},{0,3},{5,4},{6,5},{7,6},{4,7},{9,8},{10,9},{11,1... | collective-permute-start | bytes 1572872 | tf_op jit(solution)/shard_map/ppermute | solution.py:25
  33.8 43.4 %collective-permute-start.1 = (bf16[128,2048]{1,0:T(8,128)(2,1)}, bf16[128,2048]{1,0:T(8,128)(2,1)S(1)}, u32[]{:S(2)}, u32[]{:S(2)}) collective-permute-start(bf16[128,2048]{1,0:T(8,128)(2,1)} %get-tuple-element.18.refs_4_.refs_0_), channel_id=1, source_target_pairs={{2,0},{3,1},{0,2},{1,3},{6,4},{7,5},{4,6},{5,7},{10,8},{11,9},{8,1... | collective-permute-start | bytes 1572872 | tf_op jit(solution)/shard_map/ppermute | solution.py:25
  34.6 42.6 %collective-permute-start.2 = (bf16[128,2048]{1,0:T(8,128)(2,1)}, bf16[128,2048]{1,0:T(8,128)(2,1)S(1)}, u32[]{:S(2)}, u32[]{:S(2)}) collective-permute-start(bf16[128,2048]{1,0:T(8,128)(2,1)} %get-tuple-element.18.refs_4_.refs_0_), channel_id=1, source_target_pairs={{3,0},{0,1},{1,2},{2,3},{7,4},{4,5},{5,6},{6,7},{11,8},{8,9},{9,10... | collective-permute-start | bytes 1572872 | tf_op jit(solution)/shard_map/ppermute | solution.py:25
  35.5 41.7 %collective-permute-start.3 = (bf16[128,2048]{1,0:T(8,128)(2,1)}, bf16[128,2048]{1,0:T(8,128)(2,1)}, u32[]{:S(2)}, u32[]{:S(2)}) collective-permute-start(bf16[128,2048]{1,0:T(8,128)(2,1)} %get-tuple-element.20), channel_id=1, source_target_pairs={{4,0},{0,4},{5,1},{1,5},{6,2},{2,6},{7,3},{3,7},{12,8},{8,12},{13,... | collective-permute-start | bytes 1572872 | tf_op jit(solution)/shard_map/ppermute | solution.py:25
  64.9 20.0 %collective-permute-start.8 = (bf16[128,2048]{1,0:T(8,128)(2,1)}, bf16[128,2048]{1,0:T(8,128)(2,1)S(1)}, u32[]{:S(2)}, u32[]{:S(2)}) collective-permute-start(bf16[128,2048]{1,0:T(8,128)(2,1)} %get-tuple-element.22), channel_id=1, source_target_pairs={{4,0},{0,4},{5,1},{1,5},{6,2},{2,6},{7,3},{3,7},{12,8},{8,12},{13,... | collective-permute-start | bytes 1572872 | tf_op jit(solution)/shard_map/ppermute | solution.py:25
  75.6 18.2 %collective-permute-start.9 = (bf16[256,1024]{1,0:T(8,128)(2,1)}, bf16[256,1024]{1,0:T(8,128)(2,1)S(1)}, u32[]{:S(2)}, u32[]{:S(2)}) collective-permute-start(bf16[256,1024]{1,0:T(8,128)(2,1)} %get-tuple-element.23.refs_8_), channel_id=1, source_target_pairs={{4,0},{0,4},{5,1},{1,5},{6,2},{2,6},{7,3},{3,7},{12,8},{8,12},{13,... | collective-permute-start | bytes 1572872 | tf_op jit(solution)/shard_map/ppermute | solution.py:25
  78.2 21.7 %collective-permute-start.4 = (bf16[128,2048]{1,0:T(8,128)(2,1)}, bf16[128,2048]{1,0:T(8,128)(2,1)S(1)}, u32[]{:S(2)}, u32[]{:S(2)}) collective-permute-start(bf16[128,2048]{1,0:T(8,128)(2,1)} %gate.5.refs_4_), channel_id=1, source_target_pairs={{1,0},{2,1},{3,2},{0,3},{5,4},{6,5},{7,6},{4,7},{9,8},{10,9},{11,1... | collective-permute-start | bytes 1572872 | tf_op jit(solution)/shard_map/ppermute | solution.py:25
  78.2 21.7 %collective-permute-start.5 = (bf16[128,2048]{1,0:T(8,128)(2,1)}, bf16[128,2048]{1,0:T(8,128)(2,1)S(1)}, u32[]{:S(2)}, u32[]{:S(2)}) collective-permute-start(bf16[128,2048]{1,0:T(8,128)(2,1)} %gate.5.refs_4_), channel_id=1, source_target_pairs={{2,0},{3,1},{0,2},{1,3},{6,4},{7,5},{4,6},{5,7},{10,8},{11,9},{8,1... | collective-permute-start | bytes 1572872 | tf_op jit(solution)/shard_map/ppermute | solution.py:25
  78.3 25.2 %collective-permute-start.6 = (bf16[128,2048]{1,0:T(8,128)(2,1)}, bf16[128,2048]{1,0:T(8,128)(2,1)S(1)}, u32[]{:S(2)}, u32[]{:S(2)}) collective-permute-start(bf16[128,2048]{1,0:T(8,128)(2,1)} %gate.5.refs_4_), channel_id=1, source_target_pairs={{3,0},{0,1},{1,2},{2,3},{7,4},{4,5},{5,6},{6,7},{11,8},{8,9},{9,10... | collective-permute-start | bytes 1572872 | tf_op jit(solution)/shard_map/ppermute | solution.py:25
  113.0 14.1 %collective-permute-start.10 = (bf16[1024,256]{1,0:T(8,128)(2,1)}, bf16[1024,256]{1,0:T(8,128)(2,1)S(1)}, u32[]{:S(2)}, u32[]{:S(2)}) collective-permute-start(bf16[1024,256]{1,0:T(8,128)(2,1)} %get-tuple-element.25.refs_11_), channel_id=1, source_target_pairs={{4,0},{0,4},{5,1},{1,5},{6,2},{2,6},{7,3},{3,7},{12,8},{8,12},{13,... | collective-permute-start | bytes 1572872 | tf_op jit(solution)/shard_map/ppermute | solution.py:25
  137.4 35.7 %collective-permute-start.23 = (bf16[768,1024]{1,0:T(8,128)(2,1)S(1)}, bf16[768,1024]{1,0:T(8,128)(2,1)}, u32[]{:S(2)}, u32[]{:S(2)}) collective-permute-start(bf16[768,1024]{1,0:T(8,128)(2,1)S(1)} %copy-done.1), channel_id=1, source_target_pairs={{4,0},{0,4},{5,1},{1,5},{6,2},{2,6},{7,3},{3,7},{12,8},{8,12},{13,... | collective-permute-start | bytes 4718600 | tf_op jit(solution)/shard_map/ppermute | solution.py:25
  141.7 10.8 %collective-permute-start.12 = (bf16[2,512,128]{2,1,0:T(8,128)(2,1)S(1)}, bf16[2,512,128]{2,1,0:T(8,128)(2,1)S(1)}, u32[]{:S(2)}, u32[]{:S(2)}) collective-permute-start(bf16[2,512,128]{2,1,0:T(8,128)(2,1)S(1)} %get-tuple-element.37), channel_id=1, source_target_pairs={{32,0},{48,16},{0,32},{16,48},{33,1},{49,17},{1,33},{17,49},{34,2}... | collective-permute-start | bytes 786440 | tf_op jit(solution)/shard_map/ppermute | solution.py:25
  144.1 13.3 %collective-permute-start.13 = (bf16[2,512,128]{2,1,0:T(8,128)(2,1)S(1)}, bf16[2,512,128]{2,1,0:T(8,128)(2,1)S(1)}, u32[]{:S(2)}, u32[]{:S(2)}) collective-permute-start(bf16[2,512,128]{2,1,0:T(8,128)(2,1)S(1)} %get-tuple-element.39), channel_id=1, source_target_pairs={{48,0},{0,16},{16,32},{32,48},{49,1},{1,17},{17,33},{33,49},{50,2}... | collective-permute-start | bytes 786440 | tf_op jit(solution)/shard_map/ppermute | solution.py:25
  144.1 13.3 %collective-permute-start.14 = (bf16[2,512,128]{2,1,0:T(8,128)(2,1)S(1)}, bf16[2,512,128]{2,1,0:T(8,128)(2,1)S(1)}, u32[]{:S(2)}, u32[]{:S(2)}) collective-permute-start(bf16[2,512,128]{2,1,0:T(8,128)(2,1)S(1)} %get-tuple-element.38), channel_id=1, source_target_pairs={{16,0},{32,16},{48,32},{0,48},{17,1},{33,17},{49,33},{1,49},{18,2}... | collective-permute-start | bytes 786440 | tf_op jit(solution)/shard_map/ppermute | solution.py:25
  166.4 14.2 %collective-permute-start.15 = (bf16[4,2,768,128]{3,2,1,0:T(8,128)(2,1)}, bf16[4,2,768,128]{3,2,1,0:T(8,128)(2,1)}, u32[]{:S(2)}, u32[]{:S(2)}) collective-permute-start(bf16[4,2,768,128]{3,2,1,0:T(8,128)(2,1)} %get-tuple-element.29), channel_id=1, source_target_pairs={{8,0},{0,8},{9,1},{1,9},{10,2},{2,10},{11,3},{3,11},{12,4},{4,12},... | collective-permute-start | bytes 4718600 | tf_op jit(solution)/shard_map/ppermute | solution.py:25
  180.6 6.4 %collective-permute-start.24 = (bf16[4,2,768,128]{3,2,1,0:T(8,128)(2,1)}, bf16[4,2,768,128]{3,2,1,0:T(8,128)(2,1)S(1)}, u32[]{:S(2)}, u32[]{:S(2)}) collective-permute-start(bf16[4,2,768,128]{3,2,1,0:T(8,128)(2,1)} %get-tuple-element.31), channel_id=1, source_target_pairs={{8,0},{0,8},{9,1},{1,9},{10,2},{2,10},{11,3},{3,11},{12,4},{4,12},... | collective-permute-start | bytes 4718600 | tf_op jit(solution)/shard_map/ppermute | solution.py:25
  182.5 13.5 %collective-permute-start.16 = (bf16[2,768,128]{2,1,0:T(8,128)(2,1)S(1)}, bf16[2,768,128]{2,1,0:T(8,128)(2,1)S(1)}, u32[]{:S(2)}, u32[]{:S(2)}) collective-permute-start(bf16[2,768,128]{2,1,0:T(8,128)(2,1)S(1)} %get-tuple-element.34), channel_id=1, source_target_pairs={{32,0},{48,16},{0,32},{16,48},{33,1},{49,17},{1,33},{17,49},{34,2}... | collective-permute-start | bytes 1179656 | tf_op jit(solution)/shard_map/ppermute | solution.py:25
  184.9 19.3 %collective-permute-start.17 = (bf16[2,768,128]{2,1,0:T(8,128)(2,1)S(1)}, bf16[2,768,128]{2,1,0:T(8,128)(2,1)S(1)}, u32[]{:S(2)}, u32[]{:S(2)}) collective-permute-start(bf16[2,768,128]{2,1,0:T(8,128)(2,1)S(1)} %get-tuple-element.36), channel_id=1, source_target_pairs={{48,0},{0,16},{16,32},{32,48},{49,1},{1,17},{17,33},{33,49},{50,2}... | collective-permute-start | bytes 1179656 | tf_op jit(solution)/shard_map/ppermute | solution.py:25
  184.9 19.3 %collective-permute-start.18 = (bf16[2,768,128]{2,1,0:T(8,128)(2,1)S(1)}, bf16[2,768,128]{2,1,0:T(8,128)(2,1)S(1)}, u32[]{:S(2)}, u32[]{:S(2)}) collective-permute-start(bf16[2,768,128]{2,1,0:T(8,128)(2,1)S(1)} %get-tuple-element.35), channel_id=1, source_target_pairs={{16,0},{32,16},{48,32},{0,48},{17,1},{33,17},{49,33},{1,49},{18,2}... | collective-permute-start | bytes 1179656 | tf_op jit(solution)/shard_map/ppermute | solution.py:25
  206.0 24.1 %all-to-all-start.1 = ((bf16[4,2,768,128]{3,2,1,0:T(8,128)(2,1)}), bf16[4,2,768,128]{3,2,1,0:T(8,128)(2,1)S(1)}, u32[]{:S(2)}, u32[]{:S(2)}) async-start(bf16[4,2,768,128]{3,2,1,0:T(8,128)(2,1)} %gate.7), calls=%async_computation.1 | async-start | bytes 3145728 | tf_op jit(solution)/shard_map/all_to_all | solution.py:391
  210.6 20.4 %collective-permute-start.21 = (bf16[1024,128]{1,0:T(8,128)(2,1)S(1)}, bf16[1024,128]{1,0:T(8,128)(2,1)S(1)}, u32[]{:S(2)}, u32[]{:S(2)}) collective-permute-start(bf16[1024,128]{1,0:T(8,128)(2,1)S(1)} %copy-done.15), channel_id=1, source_target_pairs={{0,0},{4,132},{64,64},{68,196},{1,1},{5,133},{65,65},{69,197},{2,2... | collective-permute-start | bytes 786440 | tf_op jit(solution)/shard_map/ppermute | solution.py:35
  215.9 15.2 %collective-permute-start.22 = (bf16[1024,128]{1,0:T(8,128)(2,1)S(1)}, bf16[1024,128]{1,0:T(8,128)(2,1)S(1)}, u32[]{:S(2)}, u32[]{:S(2)}) collective-permute-start(bf16[1024,128]{1,0:T(8,128)(2,1)S(1)} %copy-done.15), channel_id=1, source_target_pairs={{128,0},{132,132},{192,64},{196,196},{129,1},{133,133},{193,65},{1... | collective-permute-start | bytes 786440 | tf_op jit(solution)/shard_map/ppermute | solution.py:35
  216.6 22.9 %collective-permute-start.19 = (bf16[1024,128]{1,0:T(8,128)(2,1)S(1)}, bf16[1024,128]{1,0:T(8,128)(2,1)S(1)}, u32[]{:S(2)}, u32[]{:S(2)}) collective-permute-start(bf16[1024,128]{1,0:T(8,128)(2,1)S(1)} %copy-done.14), channel_id=1, source_target_pairs={{0,64},{4,196},{64,0},{68,132},{1,65},{5,197},{65,1},{69,133},{2,6... | collective-permute-start | bytes 786440 | tf_op jit(solution)/shard_map/ppermute | solution.py:35
  217.9 21.6 %collective-permute-start.20 = (bf16[1024,128]{1,0:T(8,128)(2,1)S(1)}, bf16[1024,128]{1,0:T(8,128)(2,1)S(1)}, u32[]{:S(2)}, u32[]{:S(2)}) collective-permute-start(bf16[1024,128]{1,0:T(8,128)(2,1)S(1)} %copy-done.14), channel_id=1, source_target_pairs={{128,64},{132,196},{192,0},{196,132},{129,65},{133,197},{193,1},{1... | collective-permute-start | bytes 786440 | tf_op jit(solution)/shard_map/ppermute | solution.py:35
  232.5 23.0 %collective-permute-start.27 = (bf16[1024,128]{1,0:T(8,128)(2,1)}, bf16[1024,128]{1,0:T(8,128)(2,1)S(1)}, u32[]{:S(2)}, u32[]{:S(2)}) collective-permute-start(bf16[1024,128]{1,0:T(8,128)(2,1)} %gate.9), channel_id=1, source_target_pairs={{0,4},{4,128},{64,68},{68,192},{1,5},{5,129},{65,69},{69,193},{2,6... | collective-permute-start | bytes 786440 | tf_op jit(solution)/shard_map/ppermute | solution.py:35
  237.5 18.0 %collective-permute-start.28 = (bf16[1024,128]{1,0:T(8,128)(2,1)}, bf16[1024,128]{1,0:T(8,128)(2,1)S(1)}, u32[]{:S(2)}, u32[]{:S(2)}) collective-permute-start(bf16[1024,128]{1,0:T(8,128)(2,1)} %gate.9), channel_id=1, source_target_pairs={{128,4},{132,128},{192,68},{196,192},{129,5},{133,129},{193,69},{1... | collective-permute-start | bytes 786440 | tf_op jit(solution)/shard_map/ppermute | solution.py:35
  240.9 14.6 %collective-permute-start.25 = (bf16[1024,128]{1,0:T(8,128)(2,1)}, bf16[1024,128]{1,0:T(8,128)(2,1)S(1)}, u32[]{:S(2)}, u32[]{:S(2)}) collective-permute-start(bf16[1024,128]{1,0:T(8,128)(2,1)} %gate.8), channel_id=1, source_target_pairs={{0,68},{4,192},{64,4},{68,128},{1,69},{5,193},{65,5},{69,129},{2,7... | collective-permute-start | bytes 786440 | tf_op jit(solution)/shard_map/ppermute | solution.py:35
  247.6 12.1 %collective-permute-start.26 = (bf16[1024,128]{1,0:T(8,128)(2,1)}, bf16[1024,128]{1,0:T(8,128)(2,1)S(1)}, u32[]{:S(2)}, u32[]{:S(2)}) collective-permute-start(bf16[1024,128]{1,0:T(8,128)(2,1)} %gate.8), channel_id=1, source_target_pairs={{128,68},{132,192},{192,4},{196,128},{129,69},{133,193},{193,5},{1... | collective-permute-start | bytes 786440 | tf_op jit(solution)/shard_map/ppermute | solution.py:35
  (28 other events, 112.4 us)
Sparse Core Ops, SparseCore 0:
  17.4 59.4 all-gather.2
  106.7 50.0 all-gather.4
